TPU v7x, 256 devices: a whole 4x4x8 slice. The times are simulated.
256 devices in a mesh: dom: 256 (over z, y, x, core).
Axes of the slice: x: 4, y: 4, z: 8, core: 2. Of those that a mesh axis runs over, the one named last changes fastest.
Arguments:
- nodes: bfloat16 [262144, 128], P('dom'), may hold values from -6 to 6
- fine_edges: bfloat16 [2097152, 128], P('dom'), may hold values from -6 to 6
- fine_recv: int32 [16384, 128], P('dom'), may hold values from 0 to 127
- fine_send: int32 [16384, 128], P('dom'), may hold values from 0 to 1535
- fine_live: int32 [16384, 128], P('dom'), may hold values 0 or 1
- bound_rows: int32 [256, 512], P('dom'), may hold values from 0 to 1023
- cluster: int32 [262144], P('dom'), may hold values from 0 to 1023
- coarse_edges: bfloat16 [524288, 128], P('dom'), may hold values from -6 to 6
- coarse_recv: int32 [4096, 128], P('dom'), may hold values from 0 to 127
- coarse_send: int32 [4096, 128], P('dom'), may hold values from 0 to 1151, as said below
- coarse_live: int32 [4096, 128], P('dom'), may hold values 0 or 1
- coarse_bound: int32 [256, 128], P('dom'), may hold values from 0 to 1023
- edge_in: bfloat16 [3, 3, 128, 128], replicated, may hold values from -0.5 to 0.5
- edge_out: bfloat16 [3, 128, 128], replicated, may hold values from -0.5 to 0.5
- node_in: bfloat16 [3, 256, 128], replicated, may hold values from -0.375 to 0.375
- node_out: bfloat16 [3, 128, 128], replicated, may hold values from -0.5 to 0.5
Outputs:
- latents_out: bfloat16 [262144, 128], P('dom')
Inputs may be any that keep to these rules, and one draw needn't show every extreme that they name: `coarse_send`: each coarse slot's sender lies in the lookup of its partition.
All inputs are finite; a program needn't handle non-finite values. No bound on the sum of `fine_live` or of `coarse_live` on one device may be relied on, other than what follows from the above.
Results may differ from a plain program's by a relative error of at most 0.015.
Values may be sent and summed in bfloat16 or wider, within the bound.
A program may use at most 64 MiB of HBM per device.

v0:
```python
import jax
import jax.numpy as jnp
from jax import lax
from jax.sharding import PartitionSpec as P


def partner_2(block, axis, apart):
    count = lax.axis_size(axis)
    route = []
    for low in range(count):
        high = low | 1 << apart
        if high != low and high < count:
            route += [(low, high), (high, low)]
    return lax.ppermute(block, axis, route)


def extended_2(cells, sides, width):
    for axis, dim in sides:
        count = lax.axis_size(axis)
        head = lax.slice_in_dim(cells, 0, width, axis=dim)
        tail = lax.slice_in_dim(cells, cells.shape[dim] - width, cells.shape[dim], axis=dim)
        cells = jnp.concatenate(
            [
                lax.ppermute(tail, axis, [(i, (i + 1) % count) for i in range(count)]),
                cells,
                lax.ppermute(head, axis, [((i + 1) % count, i) for i in range(count)]),
            ],
            axis=dim,
        )
    return cells


def passed_along(block, axis, distance):
    devices = range(lax.axis_size(axis))
    route = [((i - distance) % len(devices), i) for i in devices]
    return lax.ppermute(block, axis, route)


def layer_norm(values):
    center = jnp.mean(values, axis=-1, keepdims=True)
    spread = jnp.mean(jnp.square(values - center), axis=-1, keepdims=True)
    return (values - center) * lax.rsqrt(spread + 1e-05)


def pick_rows(table, indices):
    columns = jnp.arange(table.shape[0], dtype=jnp.int32)
    selector = (indices[:, None] == columns[None, :]).astype(jnp.bfloat16)
    return jnp.dot(selector, table, preferred_element_type=jnp.float32).astype(jnp.bfloat16)


def process(
    own_nodes,
    lookup,
    edge_latent,
    receiver_slot,
    sender,
    live_mask,
    w_edge,
    w_message,
    w_node,
    w_update,
):
    tile_count = receiver_slot.shape[0]
    block_count = own_nodes.shape[0] // 128
    per_block = tile_count // block_count
    width = own_nodes.shape[1]
    slots = jnp.arange(128, dtype=jnp.int32)
    onehot = (receiver_slot[:, :, None] == slots[None, None, :]).astype(jnp.bfloat16)
    node_blocks = own_nodes.reshape(block_count, 128, width)
    recv_rows = jnp.einsum(
        "bpsn,bnf->bpsf",
        onehot.reshape(block_count, per_block, 128, 128),
        node_blocks,
        preferred_element_type=jnp.float32,
    ).astype(jnp.bfloat16)
    from_recv = jnp.dot(recv_rows.reshape(-1, width), w_edge[0], preferred_element_type=jnp.float32)

    def sender_block(block_senders):
        return pick_rows(lookup, block_senders)

    send_rows = lax.map(sender_block, sender.reshape(block_count, per_block * 128))
    from_send = jnp.dot(send_rows.reshape(-1, width), w_edge[1], preferred_element_type=jnp.float32)
    from_edge = jnp.dot(edge_latent, w_edge[2], preferred_element_type=jnp.float32)
    summed = from_recv + from_send + from_edge
    active = jnp.maximum(summed, 0.0).astype(jnp.bfloat16)
    message = layer_norm(jnp.dot(active, w_message, preferred_element_type=jnp.float32)).astype(
        jnp.bfloat16
    )
    new_edges = (edge_latent.astype(jnp.float32) + message.astype(jnp.float32)).astype(jnp.bfloat16)
    selector = onehot * (live_mask[:, :, None] == 1).astype(jnp.bfloat16)
    per_tile = jnp.einsum(
        "ten,tef->tnf",
        selector,
        message.reshape(tile_count, 128, -1),
        preferred_element_type=jnp.float32,
    )
    aggregate = (
        per_tile.reshape(-1, per_block, 128, width).sum(axis=1).reshape(own_nodes.shape[0], width)
    )
    joined = jnp.concatenate([own_nodes, aggregate.astype(jnp.bfloat16)], axis=1)
    hidden = jnp.maximum(jnp.dot(joined, w_node, preferred_element_type=jnp.float32), 0.0).astype(
        jnp.bfloat16
    )
    updated = (
        own_nodes.astype(jnp.float32)
        + layer_norm(jnp.dot(hidden, w_update, preferred_element_type=jnp.float32))
    ).astype(jnp.bfloat16)
    return (updated, new_edges)


def assemble_updated(quarter):
    assembled = quarter[None]
    for which_bit in range(2):
        partner = partner_2(assembled, "dom", which_bit)
        upper_side = lax.axis_index("dom") // (1 << which_bit) % 2
        assembled = jnp.where(
            upper_side == 0,
            jnp.concatenate([assembled, partner], axis=0),
            jnp.concatenate([partner, assembled], axis=0),
        )
    return assembled.reshape(-1, assembled.shape[-1])


def local(
    nodes,
    fine_edges,
    fine_recv,
    fine_send,
    fine_live,
    bound_rows,
    cluster,
    coarse_edges,
    coarse_recv,
    coarse_send,
    coarse_live,
    coarse_bound,
    edge_in,
    edge_out,
    node_in,
    node_out,
):
    node_total = nodes.shape[0]
    quarter_rows = node_total // 4
    halo_rows = bound_rows.shape[1] // 2
    coarse_halo = coarse_bound.shape[1] // 2
    position = lax.axis_index("dom") % 4
    cluster_columns = jnp.arange(node_total, dtype=jnp.int32)
    cluster_onehot = (cluster[:, None] == cluster_columns[None, :]).astype(jnp.bfloat16)

    def fine_layer(node_state, edge_state, layer_index):
        outgoing = pick_rows(node_state, bound_rows[0])
        extended = extended_2(outgoing, (("dom", 0),), halo_rows)
        lookup = jnp.concatenate([node_state, extended[:halo_rows], extended[-halo_rows:]], axis=0)
        return process(
            node_state,
            lookup,
            edge_state,
            fine_recv,
            fine_send,
            fine_live,
            edge_in[layer_index],
            edge_out[layer_index],
            node_in[layer_index],
            node_out[layer_index],
        )

    node_state, edge_state = fine_layer(nodes, fine_edges, 0)
    cluster_sums = jnp.einsum(
        "nc,nf->cf", cluster_onehot, node_state, preferred_element_type=jnp.float32
    )
    counts = jnp.sum(cluster_onehot.astype(jnp.float32), axis=0)
    for which_bit in range(2):
        other_sums, other_counts = partner_2((cluster_sums, counts), "dom", which_bit)
        cluster_sums = cluster_sums + other_sums
        counts = counts + other_counts
    group_nodes = (cluster_sums / jnp.maximum(counts, 1.0)[:, None]).astype(jnp.bfloat16)
    own_quarter = lax.dynamic_slice_in_dim(group_nodes, position * quarter_rows, quarter_rows, 0)
    coarse_out = pick_rows(group_nodes, coarse_bound[0])
    coarse_from_left = passed_along(coarse_out[coarse_halo:], "dom", 4)
    coarse_from_right = passed_along(coarse_out[:coarse_halo], "dom", -4)
    coarse_lookup = jnp.concatenate([group_nodes, coarse_from_left, coarse_from_right], axis=0)
    new_quarter, unused = process(
        own_quarter,
        coarse_lookup,
        coarse_edges,
        coarse_recv,
        coarse_send,
        coarse_live,
        edge_in[1],
        edge_out[1],
        node_in[1],
        node_out[1],
    )
    coarse_new = assemble_updated(new_quarter)
    lifted = jnp.dot(cluster_onehot, coarse_new, preferred_element_type=jnp.float32)
    node_state = (node_state.astype(jnp.float32) + lifted).astype(jnp.bfloat16)
    final_state, unused = fine_layer(node_state, edge_state, 2)
    return final_state


def solution(mesh):
    in_specs = (
        P("dom", None),
        P("dom", None),
        P("dom", None),
        P("dom", None),
        P("dom", None),
        P("dom", None),
        P("dom"),
        P("dom", None),
        P("dom", None),
        P("dom", None),
        P("dom", None),
        P("dom", None),
        P(),
        P(),
        P(),
        P(),
    )
    out_specs = P("dom", None)
    return jax.shard_map(local, mesh=mesh, in_specs=in_specs, out_specs=out_specs, check_vma=False)
```

profile of v0, /device:TPU:0, one launch (start us, length us, event | category | flops | bytes accessed | tf_op | source)
XLA Modules:
  0.0 141.7 jit_solution(12209026832331046734)
XLA Ops:
  0.0 1.5 %fusion.54 = bf16[512,128]{1,0:T(8,128)(2,1)S(1)} fusion(bf16[1024,128]{1,0:T(8,128)(2,1)} %param.22, s32[512]{0:T(512)} %bitcast.198), kind=kOutput, calls=%fused_computation.75 | convolution fusion | flops 134807552 | bytes 395264 | tf_op jit(solution)/shard_map/dot_general | solution.py:48
  1.6 8.3 %collective-permute-start.1 = (bf16[256,128]{1,0:T(8,128)(2,1)S(1)}, bf16[256,128]{1,0:T(8,128)(2,1)S(1)}, u32[]{:S(2)}, u32[]{:S(2)}) collective-permute-start(bf16[256,128]{1,0:T(8,128)(2,1)S(1)} %get-tuple-element.101), channel_id=1, source_target_pairs={{1,0},{2,1},{3,2},{4,3},{5,4},{6,5},{7,6},{8,7},{9,8},{10,9},{11,1... | collective-permute-start | bytes 196616 | tf_op jit(solution)/shard_map/ppermute | solution.py:26
  9.9 2.9 %fusion.39 = bf16[8,8,128,128]{3,2,1,0:T(8,128)(2,1)S(1)} fusion(bf16[8,128,128,1]{2,1,3,0:T(8,128)(2,1)} %bitcast.186, s32[8,8,128]{2,1,0:T(8,128)} %bitcast.196), kind=kOutput, calls=%fused_computation.61 | convolution fusion | flops 270532608 | bytes 2392064 | tf_op jit(solution)/shard_map/bpsn,bnf->bpsf/dot_general | solution.py:70
  12.9 3.4 %fusion.128 = f32[8192,128]{1,0:T(8,128)} fusion(bf16[8192,128]{1,0:T(8,128)(2,1)S(1)} %bitcast.182, bf16[3,3,128,128]{3,2,1,0:T(8,128)(2,1)} %param.34), kind=kOutput, calls=%fused_computation.148 | convolution fusion | flops 268435456 | bytes 6324224 | tf_op jit(solution)/shard_map/dot_general | solution.py:76
  16.7 10.2 %while.30 = (s32[]{:T(128)}, bf16[8,1024,128]{2,1,0:T(8,128)(2,1)S(1)}, s32[8,1024]{1,0:T(8,128)S(1)}, bf16[1536,128]{1,0:T(8,128)(2,1)S(1)}, s32[]{:T(128)}) while((s32[]{:T(128)}, bf16[8,1024,128]{2,1,0:T(8,128)(2,1)S(1)}, s32[8,1024]{1,0:T(8,128)S(1)}, bf16[1536,128]{1,0:T(8,128)(2,1)S(1)}, s32[]{:T(128)}) %tuple.53), condition=%wide.region_1.2_spmd, body=%wide.region_0.1_spmd.sunk | while | flops 404357120 | bytes 667717 | solution.py:81
  18.0 1.2 fusion.219
  19.3 1.2 fusion.219
  20.5 1.2 fusion.219
  26.9 4.8 %convolution_add_fusion.3 = f32[8192,128]{1,0:T(8,128)} fusion(f32[8192,128]{1,0:T(8,128)} %fusion.128, bf16[8192,128]{1,0:T(8,128)(2,1)S(1)} %bitcast.180, bf16[3,3,128,128]{3,2,1,0:T(8,128)(2,1)} %param.34), kind=kOutput, calls=%fused_computation.26 | convolution fusion | flops 269484032 | bytes 10518528 | tf_op jit(solution)/shard_map/dot_general | solution.py:82
  31.7 6.2 %fusion.166 = (f32[8192]{0:T(1024)S(1)}, f32[8192,128]{1,0:T(8,128)}) fusion(bf16[3,128,128]{2,1,0:T(8,128)(2,1)} %param.35, f32[8192,128]{1,0:T(8,128)} %convolution_add_fusion.3, bf16[8192,128]{1,0:T(8,128)(2,1)} %param.23, bf16[3,3,128,128]{3,2,1,0:T(8,128)(2,1)} %param.34), kind=kOutput, calls=%fused_computation.196 | convolution fusion | flops 541057024 | bytes 10584064 | tf_op jit(solution)/shard_map/dot_general | solution.py:86
  37.9 4.2 %multiply_reduce_fusion.1 = f32[8192]{0:T(1024)S(1)} fusion(f32[8192,128]{1,0:T(8,128)} %get-tuple-element.105, f32[8192]{0:T(1024)S(1)} %broadcast_multiply_fusion.1), kind=kLoop, calls=%fused_computation.40 | loop fusion | flops 3137536 | bytes 4259840 | tf_op jit(solution)/shard_map/reduce_sum | solution.py:41
  42.1 4.5 %multiply_convert_fusion.1 = bf16[8192,128]{1,0:T(8,128)(2,1)S(1)} fusion(f32[8192,128]{1,0:T(8,128)S(1)} %copy-done.2, f32[8192]{0:T(1024)S(1)} %add_rsqrt_fusion.1, f32[8192]{0:T(1024)S(1)} %broadcast_multiply_fusion.1), kind=kLoop, calls=%fused_computation.39 | loop fusion | flops 3145728 | bytes 6356992 | tf_op jit(solution)/shard_map/convert_element_type | solution.py:86
  48.1 1.5 %fusion.169 = (f32[1024]{0:T(1024)S(1)}, f32[1024,128]{1,0:T(8,128)S(1)}) fusion(bf16[3,128,128]{2,1,0:T(8,128)(2,1)} %param.37, bf16[1024,128]{1,0:T(8,128)(2,1)S(1)} %bitcast.202, bf16[1024,128]{1,0:T(8,128)(2,1)S(1)} %copy-done.4, bf16[3,256,128]{2,1,0:T(8,128)(2,1)} %param.36), kind=kOutput, calls=%fused_computation.197 | convolution fusion | flops 102104064 | bytes 1150976 | tf_op jit(solution)/shard_map/dot_general | solution.py:106
  50.3 1.4 fusion.21
  52.0 1.9 %collective-permute-done.2 = f32[1024,128]{1,0:T(8,128)S(1)} collective-permute-done((f32[1024,128]{1,0:T(8,128)S(1)}, f32[1024,128]{1,0:T(8,128)S(1)}, u32[]{:S(2)}, u32[]{:S(2)}) %collective-permute-start.2) | collective-permute-done | bytes 524320 | tf_op jit(solution)/shard_map/ppermute | solution.py:14
  55.9 2.0 %collective-permute-start.5 = (f32[1024]{0:T(1024)S(1)}, f32[1024]{0:T(1024)S(1)}, u32[]{:S(2)}, u32[]{:S(2)}) collective-permute-start(f32[1024]{0:T(1024)S(1)} %add.132), channel_id=1, source_target_pairs={{0,2},{2,0},{1,3},{3,1},{4,6},{6,4},{5,7},{7,5},{8,10},{10,8},{9,1... | collective-permute-start | bytes 12296 | tf_op jit(solution)/shard_map/ppermute | solution.py:14
  57.9 10.2 %collective-permute-done.5 = f32[1024]{0:T(1024)S(1)} collective-permute-done((f32[1024]{0:T(1024)S(1)}, f32[1024]{0:T(1024)S(1)}, u32[]{:S(2)}, u32[]{:S(2)}) %collective-permute-start.5) | collective-permute-done | bytes 4128 | tf_op jit(solution)/shard_map/ppermute | solution.py:14
  68.8 7.7 %collective-permute-start.7 = (bf16[64,128]{1,0:T(8,128)(2,1)S(1)}, bf16[64,128]{1,0:T(8,128)(2,1)S(1)}, u32[]{:S(2)}, u32[]{:S(2)}) collective-permute-start(bf16[64,128]{1,0:T(8,128)(2,1)S(1)} %get-tuple-element.103), channel_id=1, source_target_pairs={{4,0},{5,1},{6,2},{7,3},{8,4},{9,5},{10,6},{11,7},{12,8},{13,9},{1... | collective-permute-start | bytes 49160 | tf_op jit(solution)/shard_map/ppermute | solution.py:36
  78.2 2.1 %while.31 = (s32[]{:T(128)}, bf16[2,1024,128]{2,1,0:T(8,128)(2,1)S(1)}, s32[2,1024]{1,0:T(2,128)S(1)}, bf16[1152,128]{1,0:T(8,128)(2,1)S(1)}, s32[]{:T(128)}) while((s32[]{:T(128)}, bf16[2,1024,128]{2,1,0:T(8,128)(2,1)S(1)}, s32[2,1024]{1,0:T(2,128)S(1)}, bf16[1152,128]{1,0:T(8,128)(2,1)S(1)}, s32[]{:T(128)}) %tuple.56), condition=%wide.region_9.10_spmd, body=%wide.region_8.9_spmd.sunk | while | flops 303300608 | bytes 569413 | solution.py:81
  81.4 1.4 fusion.174
  84.4 1.3 fusion.177
  87.8 5.3 %collective-permute-done.9 = bf16[2,256,128]{2,1,0:T(8,128)(2,1)S(1)} collective-permute-done((bf16[2,256,128]{2,1,0:T(8,128)(2,1)S(1)}, bf16[2,256,128]{2,1,0:T(8,128)(2,1)S(1)}, u32[]{:S(2)}, u32[]{:S(2)}) %collective-permute-start.9) | collective-permute-done | bytes 131104 | tf_op jit(solution)/shard_map/ppermute | solution.py:14
  94.7 7.2 %collective-permute-start.11 = (bf16[256,128]{1,0:T(8,128)(2,1)S(1)}, bf16[256,128]{1,0:T(8,128)(2,1)S(1)}, u32[]{:S(2)}, u32[]{:S(2)}) collective-permute-start(bf16[256,128]{1,0:T(8,128)(2,1)S(1)} %get-tuple-element.99), channel_id=1, source_target_pairs={{1,0},{2,1},{3,2},{4,3},{5,4},{6,5},{7,6},{8,7},{9,8},{10,9},{11,1... | collective-permute-start | bytes 196616 | tf_op jit(solution)/shard_map/ppermute | solution.py:26
  101.8 1.9 %fusion.40 = bf16[8,8,128,128]{3,2,1,0:T(8,128)(2,1)S(1)} fusion(bf16[8,128,128,1]{2,1,3,0:T(8,128)(2,1)S(1)} %bitcast.187, s32[8,8,128]{2,1,0:T(8,128)S(1)} %bitcast.197), kind=kOutput, calls=%fused_computation.62 | convolution fusion | flops 270532608 | bytes 2392064 | tf_op jit(solution)/shard_map/bpsn,bnf->bpsf/dot_general | solution.py:70
  103.7 3.4 %fusion.114 = f32[8192,128]{1,0:T(8,128)} fusion(bf16[8192,128]{1,0:T(8,128)(2,1)S(1)} %bitcast.183, bf16[3,3,128,128]{3,2,1,0:T(8,128)(2,1)} %param.34), kind=kOutput, calls=%fused_computation.136 | convolution fusion | flops 268435456 | bytes 6324224 | tf_op jit(solution)/shard_map/dot_general | solution.py:76
  107.4 10.2 %while.32 = (s32[]{:T(128)}, bf16[8,1024,128]{2,1,0:T(8,128)(2,1)S(1)}, s32[8,1024]{1,0:T(8,128)S(1)}, bf16[1536,128]{1,0:T(8,128)(2,1)S(1)}, s32[]{:T(128)}) while((s32[]{:T(128)}, bf16[8,1024,128]{2,1,0:T(8,128)(2,1)S(1)}, s32[8,1024]{1,0:T(8,128)S(1)}, bf16[1536,128]{1,0:T(8,128)(2,1)S(1)}, s32[]{:T(128)}) %tuple.62), condition=%wide.region_16.17_spmd, body=%wide.region_15.16_spmd.sunk | while | flops 404357120 | bytes 667717 | solution.py:81
  116.4 1.2 fusion.223
  117.6 4.8 %convolution_add_fusion.1 = f32[8192,128]{1,0:T(8,128)} fusion(f32[8192,128]{1,0:T(8,128)} %fusion.114, bf16[8192,128]{1,0:T(8,128)(2,1)S(1)} %bitcast.179, bf16[3,3,128,128]{3,2,1,0:T(8,128)(2,1)} %param.34), kind=kOutput, calls=%fused_computation.23 | convolution fusion | flops 269484032 | bytes 10518528 | tf_op jit(solution)/shard_map/dot_general | solution.py:82
  122.4 6.8 %fusion.182 = (f32[8192]{0:T(1024)S(1)}, f32[8192,128]{1,0:T(8,128)}) fusion(bf16[3,128,128]{2,1,0:T(8,128)(2,1)} %param.35, f32[8192,128]{1,0:T(8,128)} %convolution_add_fusion.1, bf16[8192,128]{1,0:T(8,128)(2,1)} %copy-done.3, bf16[8192,128]{1,0:T(8,128)(2,1)} %param.23, bf16[3,3,128,128]{3,2,1,0:T(8,128)(2,1)} %param.34), kind=kOutput, calls=%fused_computation.200 | convolution fusion | flops 545251328 | bytes 12681216 | tf_op jit(solution)/shard_map/dot_general | solution.py:86
  129.2 4.2 %multiply_reduce_fusion = f32[8192]{0:T(1024)S(1)} fusion(f32[8192,128]{1,0:T(8,128)} %get-tuple-element.113, f32[8192]{0:T(1024)S(1)} %broadcast_multiply_fusion), kind=kLoop, calls=%fused_computation.32 | loop fusion | flops 3137536 | bytes 4259840 | tf_op jit(solution)/shard_map/reduce_sum | solution.py:41
  133.4 4.5 %multiply_convert_fusion = bf16[8192,128]{1,0:T(8,128)(2,1)S(1)} fusion(f32[8192,128]{1,0:T(8,128)S(1)} %copy-done.1, f32[8192]{0:T(1024)S(1)} %add_rsqrt_fusion, f32[8192]{0:T(1024)S(1)} %broadcast_multiply_fusion), kind=kLoop, calls=%fused_computation.31 | loop fusion | flops 3145728 | bytes 6356992 | tf_op jit(solution)/shard_map/convert_element_type | solution.py:86
  138.7 1.4 fusion.185
  (136 shorter events, 33.1 us)
Async XLA Ops:
  0.0 81.4 %copy-start = (bf16[2048,128]{1,0:T(8,128)(2,1)S(1)}, bf16[2048,128]{1,0:T(8,128)(2,1)}, u32[]{:S(2)}) copy-start(bf16[2048,128]{1,0:T(8,128)(2,1)} %param.29) | copy-start | bytes 1572868
  1.6 14.8 %collective-permute-start = (bf16[256,128]{1,0:T(8,128)(2,1)S(1)}, bf16[256,128]{1,0:T(8,128)(2,1)S(1)}, u32[]{:S(2)}, u32[]{:S(2)}) collective-permute-start(bf16[256,128]{1,0:T(8,128)(2,1)S(1)} %get-tuple-element.100), channel_id=1, source_target_pairs={{0,1},{1,2},{2,3},{3,4},{4,5},{5,6},{6,7},{7,8},{8,9},{9,10},{10,1... | collective-permute-start | bytes 196616 | tf_op jit(solution)/shard_map/ppermute | solution.py:24
  1.6 14.7 %collective-permute-start.1 = (bf16[256,128]{1,0:T(8,128)(2,1)S(1)}, bf16[256,128]{1,0:T(8,128)(2,1)S(1)}, u32[]{:S(2)}, u32[]{:S(2)}) collective-permute-start(bf16[256,128]{1,0:T(8,128)(2,1)S(1)} %get-tuple-element.101), channel_id=1, source_target_pairs={{1,0},{2,1},{3,2},{4,3},{5,4},{6,5},{7,6},{8,7},{9,8},{10,9},{11,1... | collective-permute-start | bytes 196616 | tf_op jit(solution)/shard_map/ppermute | solution.py:26
  12.8 3.5 %copy-start.7 = (s32[64,128]{1,0:T(8,128)S(1)}, s32[64,128]{1,0:T(8,128)}, u32[]{:S(2)}) copy-start(s32[64,128]{1,0:T(8,128)} %param.26) | copy-start | bytes 98308
  12.8 3.5 %copy-start.8 = (s32[64,128]{1,0:T(8,128)S(1)}, s32[64,128]{1,0:T(8,128)}, u32[]{:S(2)}) copy-start(s32[64,128]{1,0:T(8,128)} %param.25) | copy-start | bytes 98308
  12.9 3.5 %copy-start.4 = (bf16[1024,128]{1,0:T(8,128)(2,1)S(1)}, bf16[1024,128]{1,0:T(8,128)(2,1)}, u32[]{:S(2)}) copy-start(bf16[1024,128]{1,0:T(8,128)(2,1)} %param.22) | copy-start | bytes 786436
  37.9 4.2 %copy-start.2 = (f32[8192,128]{1,0:T(8,128)S(1)}, f32[8192,128]{1,0:T(8,128)}, u32[]{:S(2)}) copy-start(f32[8192,128]{1,0:T(8,128)} %get-tuple-element.105) | copy-start | bytes 12582916
  42.1 4.6 %copy-start.12 = (s32[64,128]{1,0:T(8,128)S(1)}, s32[64,128]{1,0:T(8,128)}, u32[]{:S(2)}) copy-start(s32[64,128]{1,0:T(8,128)} %param.24) | copy-start | bytes 98308
  46.7 1.4 copy-start.3
  48.1 2.2 %copy-start.14 = (s32[1024]{0:T(1024)S(1)}, s32[1024]{0:T(1024)}, u32[]{:S(2)}) copy-start(s32[1024]{0:T(1024)} %param.28) | copy-start | bytes 12292
  49.9 8.0 %copy-start.10 = (s32[16,128]{1,0:T(8,128)S(1)}, s32[16,128]{1,0:T(8,128)}, u32[]{:S(2)}) copy-start(s32[16,128]{1,0:T(8,128)} %param.32) | copy-start | bytes 24580
  49.9 8.0 %copy-start.11 = (s32[16,128]{1,0:T(8,128)S(1)}, s32[16,128]{1,0:T(8,128)}, u32[]{:S(2)}) copy-start(s32[16,128]{1,0:T(8,128)} %param.31) | copy-start | bytes 24580
  50.3 3.6 %copy-start.5 = (bf16[1024,128]{1,0:T(8,128)(2,1)}, bf16[1024,128]{1,0:T(8,128)(2,1)S(1)}, u32[]{:S(2)}) copy-start(bf16[1024,128]{1,0:T(8,128)(2,1)S(1)} %add_convert_fusion.5) | copy-start | bytes 786436
  50.3 18.1 %copy-start.17 = (s32[1,128]{1,0:T(1,128)S(1)}, s32[1,128]{1,0:T(1,128)}, u32[]{:S(2)}) copy-start(s32[1,128]{1,0:T(1,128)} %param.33) | copy-start | bytes 1540
  51.7 24.8 %copy-start.9 = (s32[16,128]{1,0:T(8,128)S(1)}, s32[16,128]{1,0:T(8,128)}, u32[]{:S(2)}) copy-start(s32[16,128]{1,0:T(8,128)} %param.30) | copy-start | bytes 24580
  51.8 2.2 %collective-permute-start.2 = (f32[1024,128]{1,0:T(8,128)S(1)}, f32[1024,128]{1,0:T(8,128)S(1)}, u32[]{:S(2)}, u32[]{:S(2)}) collective-permute-start(f32[1024,128]{1,0:T(8,128)S(1)} %fusion.21), channel_id=1, source_target_pairs={{0,1},{1,0},{2,3},{3,2},{4,5},{5,4},{6,7},{7,6},{8,9},{9,8},{10,11... | collective-permute-start | bytes 1572872 | tf_op jit(solution)/shard_map/ppermute | solution.py:14
  54.0 14.1 %collective-permute-start.3 = (f32[1024,128]{1,0:T(8,128)S(1)}, f32[1024,128]{1,0:T(8,128)S(1)}, u32[]{:S(2)}, u32[]{:S(2)}) collective-permute-start(f32[1024,128]{1,0:T(8,128)S(1)} %add.130), channel_id=1, source_target_pairs={{0,2},{2,0},{1,3},{3,1},{4,6},{6,4},{5,7},{7,5},{8,10},{10,8},{9,1... | collective-permute-start | bytes 1572872 | tf_op jit(solution)/shard_map/ppermute | solution.py:14
  54.6 1.3 collective-permute-start.4
  55.9 12.3 %collective-permute-start.5 = (f32[1024]{0:T(1024)S(1)}, f32[1024]{0:T(1024)S(1)}, u32[]{:S(2)}, u32[]{:S(2)}) collective-permute-start(f32[1024]{0:T(1024)S(1)} %add.132), channel_id=1, source_target_pairs={{0,2},{2,0},{1,3},{3,1},{4,6},{6,4},{5,7},{7,5},{8,10},{10,8},{9,1... | collective-permute-start | bytes 12296 | tf_op jit(solution)/shard_map/ppermute | solution.py:14
  68.7 9.5 %collective-permute-start.6 = (bf16[64,128]{1,0:T(8,128)(2,1)S(1)}, bf16[64,128]{1,0:T(8,128)(2,1)S(1)}, u32[]{:S(2)}, u32[]{:S(2)}) collective-permute-start(bf16[64,128]{1,0:T(8,128)(2,1)S(1)} %get-tuple-element.102), channel_id=1, source_target_pairs={{252,0},{253,1},{254,2},{255,3},{0,4},{1,5},{2,6},{3,7},{4,8},{5,9... | collective-permute-start | bytes 49160 | tf_op jit(solution)/shard_map/ppermute | solution.py:36
  68.8 9.5 %collective-permute-start.7 = (bf16[64,128]{1,0:T(8,128)(2,1)S(1)}, bf16[64,128]{1,0:T(8,128)(2,1)S(1)}, u32[]{:S(2)}, u32[]{:S(2)}) collective-permute-start(bf16[64,128]{1,0:T(8,128)(2,1)S(1)} %get-tuple-element.103), channel_id=1, source_target_pairs={{4,0},{5,1},{6,2},{7,3},{8,4},{9,5},{10,6},{11,7},{12,8},{13,9},{1... | collective-permute-start | bytes 49160 | tf_op jit(solution)/shard_map/ppermute | solution.py:36
  83.5 9.6 %copy-start.6 = (bf16[1024,128]{1,0:T(8,128)(2,1)S(1)}, bf16[1024,128]{1,0:T(8,128)(2,1)}, u32[]{:S(2)}) copy-start(bf16[1024,128]{1,0:T(8,128)(2,1)} %copy-done.5) | copy-start | bytes 786436
  83.5 9.6 %copy-start.15 = (s32[1024]{0:T(1024)S(1)}, s32[1024]{0:T(1024)}, u32[]{:S(2)}) copy-start(s32[1024]{0:T(1024)} %param.28) | copy-start | bytes 12292
  84.4 9.6 %copy-start.16 = (s32[1,512]{1,0:T(1,128)S(1)}, s32[1,512]{1,0:T(1,128)}, u32[]{:S(2)}) copy-start(s32[1,512]{1,0:T(1,128)} %param.27) | copy-start | bytes 6148
  86.0 1.3 collective-permute-start.8
  87.4 5.6 %collective-permute-start.9 = (bf16[2,256,128]{2,1,0:T(8,128)(2,1)S(1)}, bf16[2,256,128]{2,1,0:T(8,128)(2,1)S(1)}, u32[]{:S(2)}, u32[]{:S(2)}) collective-permute-start(bf16[2,256,128]{2,1,0:T(8,128)(2,1)S(1)} %maximum_select_fusion.1), channel_id=1, source_target_pairs={{0,2},{2,0},{1,3},{3,1},{4,6},{6,4},{5,7},{7,5},{8,10},{10,8},{9,1... | collective-permute-start | bytes 393224 | tf_op jit(solution)/shard_map/ppermute | solution.py:14
  87.8 14.1 %copy-start.13 = (s32[64,128]{1,0:T(8,128)S(1)}, s32[64,128]{1,0:T(8,128)}, u32[]{:S(2)}) copy-start(s32[64,128]{1,0:T(8,128)} %param.24) | copy-start | bytes 98308
  94.6 12.5 %collective-permute-start.10 = (bf16[256,128]{1,0:T(8,128)(2,1)S(1)}, bf16[256,128]{1,0:T(8,128)(2,1)S(1)}, u32[]{:S(2)}, u32[]{:S(2)}) collective-permute-start(bf16[256,128]{1,0:T(8,128)(2,1)S(1)} %get-tuple-element.98), channel_id=1, source_target_pairs={{0,1},{1,2},{2,3},{3,4},{4,5},{5,6},{6,7},{7,8},{8,9},{9,10},{10,1... | collective-permute-start | bytes 196616 | tf_op jit(solution)/shard_map/ppermute | solution.py:24
  94.7 12.4 %collective-permute-start.11 = (bf16[256,128]{1,0:T(8,128)(2,1)S(1)}, bf16[256,128]{1,0:T(8,128)(2,1)S(1)}, u32[]{:S(2)}, u32[]{:S(2)}) collective-permute-start(bf16[256,128]{1,0:T(8,128)(2,1)S(1)} %get-tuple-element.99), channel_id=1, source_target_pairs={{1,0},{2,1},{3,2},{4,3},{5,4},{6,5},{7,6},{8,7},{9,8},{10,9},{11,1... | collective-permute-start | bytes 196616 | tf_op jit(solution)/shard_map/ppermute | solution.py:26
  129.2 4.2 %copy-start.1 = (f32[8192,128]{1,0:T(8,128)S(1)}, f32[8192,128]{1,0:T(8,128)}, u32[]{:S(2)}) copy-start(f32[8192,128]{1,0:T(8,128)} %get-tuple-element.113) | copy-start | bytes 12582916
where the time goes:
time: 142 us
  matrix products  70.5 us (50%)
  starting transfers between devices  26.5 us (19%)
  other arithmetic  22.1 us (16%)
  waiting for transfers between devices  19.9 us (14%)
  local copies, waits for them, and re-layouts  1.71 us (1%)
    dot_general x21, matrix products, pick_rows(): jnp.dot(selector, table, preferred_element_type=jnp.float32)  24.3 us
    ppermute x6, waiting for transfers between devices, partner_2(): return lax.ppermute(block, axis, route)  19.7 us
    ppermute x2, starting transfers between devices, extended_2(): lax.ppermute(head, axis, [((i + 1) % count, i) for i in range(count)])  15.4 us
    dot_general x3, matrix products, process(): jnp.dot(active, w_message, preferred_element_type=jnp.float32)  14.3 us
    dot_general x3, matrix products, process(): jnp.dot(send_rows.reshape(-1, width), w_edge[1], preferred_element_type=j...  10.7 us
    reduce_sum x6, other arithmetic, layer_norm(): spread = jnp.mean(jnp.square(values - center), axis=-1, keepdims=True)  9.86 us
    convert_element_type x3, other arithmetic, process(): layer_norm(jnp.dot(active, w_message, preferred_element_type=jnp.float32))  9.69 us
    dot_general x3, matrix products, process(): jnp.dot(recv_rows.reshape(-1, width), w_edge[0], preferred_element_type=j...  7.83 us
  transfers between devices with their start and end apart: 12, of which 6 were waited for; matrix products, arithmetic and copies ran while one was open for 10% of the time, Pallas kernels for 0%

commit v1 on v0

v1 whole, which is shorter than its diff:
```python
import functools

import jax
import jax.numpy as jnp
from jax import lax
from jax.experimental import pallas as pl
from jax.experimental.pallas import tpu as pltpu
from jax.sharding import PartitionSpec as P

MESH = pl.DeviceIdType.MESH
BF = jnp.bfloat16
F32 = jnp.float32
I32 = jnp.int32
SLOTS = 1024


def dot(a, b):
    return jnp.dot(a, b, preferred_element_type=F32)


def dot_nt(a, b):
    return lax.dot_general(a, b, (((1,), (1,)), ((), ())), preferred_element_type=F32)


def onehot(index, rows):
    numbers = lax.broadcasted_iota(jnp.int16, (rows, index.shape[1]), 0)
    return jnp.where(numbers == index.astype(jnp.int16), jnp.ones((), BF), jnp.zeros((), BF))


def half_of(upper, folded):
    return jnp.where(upper == 1, folded[128:], folded[:128])


def centred(weight_t):
    wide = weight_t.astype(F32)
    return (wide - jnp.mean(wide, axis=0, keepdims=True)).astype(BF)


def normalised(values):
    spread = jnp.mean(values * values, axis=0, keepdims=True)
    return values * lax.rsqrt(spread + 1e-05)


def index_row(ref, tile, tiles):
    base = pl.multiple_of(tile, 8)
    rows = ref[pl.ds(base, 8), :]
    return jnp.concatenate([rows[i : i + 1, :] for i in range(tiles)], axis=1)


def kernel(
    total,
    nodes_h,
    fine_edges_h,
    fine_recv_h,
    fine_send_h,
    fine_live_h,
    bound_h,
    cluster_h,
    coarse_edges_h,
    coarse_recv_h,
    coarse_send_h,
    coarse_live_h,
    coarse_bound_h,
    edge_in_h,
    edge_out_h,
    node_in_h,
    node_out_h,
    out_ref,
    nodes,
    fine_edges,
    fine_recv,
    fine_send,
    fine_live,
    bound,
    cluster,
    coarse_edges,
    coarse_recv,
    coarse_send,
    coarse_live,
    coarse_bound,
    edge_in,
    edge_out,
    node_in,
    node_out,
    state,
    edges_t,
    before,
    aggregate,
    recv_table,
    own_table,
    halo_table,
    halo_out,
    cluster_hot,
    count_out,
    count_in,
    part,
    part_in,
    pair_out,
    pair_in,
    coarse_table,
    coarse_out,
    coarse_in,
    coarse_new,
    load_sem,
    edge_sem,
    send_sem,
    recv_sem,
):
    me = lax.axis_index("dom")
    q = lax.rem(me, 4)
    base = me - q
    parity = lax.rem(q, 2)
    half = q // 2
    left = lax.rem(me + total - 1, total)
    right = lax.rem(me + 1, total)
    down = lax.rem(me + total - 4, total)
    up = lax.rem(me + 4, total)
    mate = [None, base + q + 1 - 2 * parity, base + q + 2 - 4 * half, base + 3 - q]

    def remote(slot, src, dst, device):
        return pltpu.make_async_remote_copy(
            src_ref=src,
            dst_ref=dst,
            send_sem=send_sem.at[slot],
            recv_sem=recv_sem.at[slot],
            device_id=(device,),
            device_id_type=MESH,
        )

    barrier = pltpu.get_barrier_semaphore()
    for other in (left, right, down, up, mate[1], mate[2], mate[3]):
        pl.semaphore_signal(barrier, inc=1, device_id=(other,), device_id_type=MESH)

    loads = {}
    for i, (name, src, dst) in enumerate(
        (
            ("nodes", nodes_h, nodes),
            ("edge_in", edge_in_h, edge_in),
            ("bound", bound_h, bound),
            ("fine_send", fine_send_h, fine_send),
            ("fine_recv", fine_recv_h, fine_recv),
            ("cluster", cluster_h, cluster),
            ("fine_live", fine_live_h, fine_live),
            ("edge_out", edge_out_h, edge_out),
            ("node_in", node_in_h, node_in),
            ("node_out", node_out_h, node_out),
            ("coarse_edges", coarse_edges_h, coarse_edges),
            ("coarse_recv", coarse_recv_h, coarse_recv),
            ("coarse_send", coarse_send_h, coarse_send),
            ("coarse_live", coarse_live_h, coarse_live),
            ("coarse_bound", coarse_bound_h, coarse_bound),
        )
    ):
        loads[name] = pltpu.make_async_copy(src, dst, load_sem.at[i])

    def edge_load(b):
        rows = pl.ds(pl.multiple_of(b * 1024, 1024), 1024)
        return pltpu.make_async_copy(fine_edges_h.at[rows], fine_edges.at[rows], edge_sem.at[b])

    for name in ("nodes", "edge_in", "bound", "fine_send", "fine_recv", "cluster"):
        loads[name].start()
    for b in range(8):
        edge_load(b).start()
    for name in loads:
        if name not in ("nodes", "edge_in", "bound", "fine_send", "fine_recv", "cluster"):
            loads[name].start()

    def own_part(layer, blocks, recv_ref, send_ref, edge_block):
        w_edge = edge_in[layer, 2].T

        def block(b, carry):
            send = index_row(send_ref, b * 8, 8)
            recv = index_row(recv_ref, b * 8, 8)
            inside = jnp.where(send < 1024, send & 511, -1)
            gathered = half_of((send >> 9) & 1, dot(own_table[...], onehot(inside, 512)))
            joined = jnp.concatenate([recv_table[b], w_edge], axis=1)
            columns = jnp.concatenate([onehot(recv, 128), edge_block(b)], axis=0)
            before[:, pl.ds(pl.multiple_of(b * 1024, 1024), 1024)] = gathered + dot(joined, columns)
            return carry

        lax.fori_loop(0, blocks, block, 0)

    def messages(layer, blocks, recv_ref, live_ref, rim_part, keep):
        w_message = centred(edge_out[layer].T)

        def block(b, carry):
            columns = pl.ds(pl.multiple_of(b * 1024, 1024), 1024)
            summed = before[:, columns] + rim_part(b)
            active = jnp.maximum(summed, 0.0).astype(BF)
            message = normalised(dot(w_message, active)).astype(BF)
            if keep:
                edges_t[:, columns] = (
                    edges_t[:, columns].astype(F32) + message.astype(F32)
                ).astype(BF)
            target = jnp.where(index_row(live_ref, b * 8, 8) == 1, index_row(recv_ref, b * 8, 8), -1)
            aggregate[b] = dot_nt(message, onehot(target, 128))
            return carry

        lax.fori_loop(0, blocks, block, 0)

    def node_update(layer, blocks, own):
        totals = jnp.concatenate([aggregate[b] for b in range(blocks)], axis=1)
        joined = jnp.concatenate([own, totals.astype(BF)], axis=0)
        hidden = jnp.maximum(dot(node_in[layer].T, joined), 0.0).astype(BF)
        change = normalised(dot(centred(node_out[layer].T), hidden))
        return (own.astype(F32) + change).astype(BF)

    def fine_tables(layer):
        own = state[...]
        table = dot(edge_in[layer, 1].T, own).astype(BF)
        own_table[:128, :] = table[:, :512]
        own_table[128:, :] = table[:, 512:]

    def recv_tables(layer, own, blocks):
        table = dot(edge_in[layer, 0].T, own).astype(BF)
        for b in range(blocks):
            recv_table[b] = table[:, b * 128 : (b + 1) * 128]

    def fine_halo(which):
        rows = bound[...]
        picked = half_of(rows >> 9, dot(own_table[...], onehot(rows & 511, 512))).astype(BF)
        halo_out[which, 0] = picked[:, :256]
        halo_out[which, 1] = picked[:, 256:]
        to_left = remote(
            2 * which,
            halo_out.at[which, 0],
            halo_table.at[which, pl.ds(128, 128)],
            left,
        )
        to_right = remote(
            2 * which + 1,
            halo_out.at[which, 1],
            halo_table.at[which, pl.ds(0, 128)],
            right,
        )
        return to_left, to_right

    def fine_rim(which):
        def rim_part(b):
            send = index_row(fine_send, b * 8, 8)
            outside = jnp.where(send >= 1024, send & 255, -1)
            return half_of((send >> 8) & 1, dot(halo_table[which], onehot(outside, 256)))

        return rim_part

    loads["nodes"].wait()
    loads["edge_in"].wait()
    loads["bound"].wait()
    state[...] = nodes[...].T
    fine_tables(0)
    copies = fine_halo(0)
    pl.semaphore_wait(barrier, 7)
    for copy in copies:
        copy.start()

    loads["cluster"].wait()
    label = index_row(cluster, 0, 8)
    cluster_hot[...] = onehot(label & 511, 512)
    members = lax.broadcasted_iota(I32, (16, 1024), 0) // 8 == (label >> 9)
    count_out[...] = dot_nt(jnp.where(members, 1.0, 0.0).astype(BF), cluster_hot[...])
    count_copies = [remote(3 + k, count_out, count_in.at[k - 1], mate[k]) for k in (1, 2, 3)]
    for copy in count_copies:
        copy.start()

    recv_tables(0, state[...], 8)
    loads["fine_send"].wait()
    loads["fine_recv"].wait()

    def first_edges(b):
        edge_load(b).wait()
        turned = fine_edges[pl.ds(pl.multiple_of(b * 1024, 1024), 1024), :].T
        edges_t[:, pl.ds(pl.multiple_of(b * 1024, 1024), 1024)] = turned
        return turned

    own_part(0, 8, fine_recv, fine_send, first_edges)
    loads["edge_out"].wait()
    loads["fine_live"].wait()
    for copy in copies:
        copy.wait()
    messages(0, 8, fine_recv, fine_live, fine_rim(0), True)
    loads["node_in"].wait()
    loads["node_out"].wait()
    state[...] = node_update(0, 8, state[...])

    for copy in count_copies:
        copy.wait()
    counts = count_out[...] + count_in[0] + count_in[1] + count_in[2]
    share = 1.0 / jnp.maximum(counts, 1.0)
    fine = state[...]
    nothing = jnp.zeros_like(fine)
    folded = jnp.concatenate(
        [jnp.where(label < 512, fine, nothing), jnp.where(label < 512, nothing, fine)], axis=0
    )
    sums = dot_nt(folded, cluster_hot[...])
    for i in range(2):
        means = (sums[i * 128 : i * 128 + 128] * share[i * 8 : i * 8 + 1]).astype(BF)
        part[0, i] = means[:, :256]
        part[1, i] = means[:, 256:]
    copy = remote(7, part.at[1 - parity], part_in, mate[1])
    copy.start()
    copy.wait()
    pair_out[...] = (part[parity].astype(F32) + part_in[...].astype(F32)).astype(BF)
    copy = remote(8, pair_out.at[1 - half], pair_in, mate[2])
    copy.start()
    copy.wait()
    quarter = (pair_out[half].astype(F32) + pair_in[...].astype(F32)).astype(BF)

    coarse_table[parity, half] = dot(edge_in[1, 1].T, quarter).astype(BF)
    copy = remote(9, coarse_table.at[parity, half], coarse_table.at[parity, half], mate[2])
    copy.start()
    recv_tables(1, quarter, 2)
    for name in ("coarse_edges", "coarse_recv", "coarse_send", "coarse_live", "coarse_bound"):
        loads[name].wait()
    copy.wait()
    copy = remote(10, coarse_table.at[parity], coarse_table.at[parity], mate[1])
    copy.start()
    copy.wait()
    for i in range(2):
        own_table[:, i * 256 : i * 256 + 256] = coarse_table[i].reshape(256, 256)
    rows = coarse_bound[...]
    coarse_out[...] = half_of(rows >> 9, dot(own_table[...], onehot(rows & 511, 512))).astype(BF)
    copies = (
        remote(11, coarse_out, coarse_in.at[1], down),
        remote(12, coarse_out, coarse_in.at[0], up),
    )
    for copy in copies:
        copy.start()

    def coarse_block(b):
        return coarse_edges[pl.ds(pl.multiple_of(b * 1024, 1024), 1024), :].T

    own_part(1, 2, coarse_recv, coarse_send, coarse_block)
    for copy in copies:
        copy.wait()
    lane = lax.broadcasted_iota(I32, (128, 128), 1)
    rim = jnp.where(lane < 64, coarse_in[1].astype(F32), coarse_in[0].astype(F32)).astype(BF)

    def coarse_rim(b):
        send = index_row(coarse_send, b * 8, 8)
        place = jnp.where(send < 1088, (send & 63) + 64, send & 63)
        return dot(rim, onehot(jnp.where(send >= 1024, place, -1), 128))

    messages(1, 2, coarse_recv, coarse_live, coarse_rim, False)
    coarse_new[parity, half] = node_update(1, 2, quarter)
    copy = remote(13, coarse_new.at[parity, half], coarse_new.at[parity, half], mate[2])
    copy.start()
    copy.wait()
    copy = remote(14, coarse_new.at[parity], coarse_new.at[parity], mate[1])
    copy.start()
    copy.wait()
    lifted = dot(coarse_new[0].reshape(256, 256), cluster_hot[:256, :])
    lifted += dot(coarse_new[1].reshape(256, 256), cluster_hot[256:, :])
    state[...] = (state[...].astype(F32) + half_of(label >> 9, lifted)).astype(BF)

    fine_tables(2)
    copies = fine_halo(1)
    for copy in copies:
        copy.start()
    recv_tables(2, state[...], 8)

    def last_edges(b):
        return edges_t[:, pl.ds(pl.multiple_of(b * 1024, 1024), 1024)]

    own_part(2, 8, fine_recv, fine_send, last_edges)
    for copy in copies:
        copy.wait()
    messages(2, 8, fine_recv, fine_live, fine_rim(1), False)
    out_ref[...] = node_update(2, 8, state[...]).T


def local(
    nodes,
    fine_edges,
    fine_recv,
    fine_send,
    fine_live,
    bound_rows,
    cluster,
    coarse_edges,
    coarse_recv,
    coarse_send,
    coarse_live,
    coarse_bound,
    edge_in,
    edge_out,
    node_in,
    node_out,
):
    args = (
        nodes,
        fine_edges,
        fine_recv,
        fine_send,
        fine_live,
        bound_rows,
        cluster.reshape(8, 128),
        coarse_edges,
        coarse_recv,
        coarse_send,
        coarse_live,
        coarse_bound,
        edge_in,
        edge_out,
        node_in,
        node_out,
    )
    vmem = pltpu.VMEM
    return pl.pallas_call(
        functools.partial(kernel, lax.axis_size("dom")),
        out_shape=jax.ShapeDtypeStruct((1024, 128), BF),
        in_specs=[pl.BlockSpec(memory_space=pl.ANY)] * len(args),
        out_specs=pl.BlockSpec(memory_space=pltpu.VMEM),
        scratch_shapes=[vmem(a.shape, a.dtype) for a in args]
        + [
            vmem((128, 1024), BF),
            vmem((128, 8192), BF),
            vmem((128, 8192), F32),
            vmem((8, 128, 128), F32),
            vmem((8, 128, 128), BF),
            vmem((256, 512), BF),
            vmem((2, 256, 256), BF),
            vmem((2, 2, 128, 256), BF),
            vmem((512, 1024), BF),
            vmem((16, 512), F32),
            vmem((3, 16, 512), F32),
            vmem((2, 2, 128, 256), BF),
            vmem((2, 128, 256), BF),
            vmem((2, 128, 256), BF),
            vmem((128, 256), BF),
            vmem((2, 2, 128, 256), BF),
            vmem((128, 128), BF),
            vmem((2, 128, 128), BF),
            vmem((2, 2, 128, 256), BF),
            pltpu.SemaphoreType.DMA((15,)),
            pltpu.SemaphoreType.DMA((8,)),
            pltpu.SemaphoreType.DMA((15,)),
            pltpu.SemaphoreType.DMA((15,)),
        ],
        compiler_params=pltpu.CompilerParams(
            collective_id=0, has_side_effects=True, vmem_limit_bytes=56 << 20
        ),
    )(*args)


def solution(mesh):
    row = P("dom", None)
    return jax.shard_map(
        local,
        mesh=mesh,
        in_specs=(row,) * 6 + (P("dom"),) + (row,) * 5 + (P(),) * 4,
        out_specs=row,
        check_vma=False,
    )
```

time: 142 us -> 59.2 us (0.42)
  the two profiles are of different devices: /device:TPU:0 before, /device:TPU:1 now
where the time goes in v1:
time: 59.2 us; the launch traced here: 59.1 us
  Pallas kernels  57.4 us (97%)
  local copies, waits for them, and re-layouts  1.67 us (3%)
    pallas_call x1, Pallas kernels, local(): pl.pallas_call(functools.partial(kernel, lax.axis_size('dom')), out_shape...  57.4 us
    unnamed x1, local copies, waits for them, and re-layouts  1.67 us

profile of v1, /device:TPU:1, one launch (start us, length us, event | category | flops | bytes accessed | tf_op | source)
XLA Modules:
  0.0 59.1 jit_solution(15851200863639638566)
XLA Ops:
  0.0 57.4 %shard_map.154 = bf16[1024,128]{1,0:T(8,128)(2,1)} custom-call(bf16[1024,128]{1,0:T(8,128)(2,1)} %nodes_h.1, bf16[8192,128]{1,0:T(8,128)(2,1)} %fine_edges_h.1, s32[64,128]{1,0:T(8,128)} %fine_recv_h.1, s32[64,128]{1,0:T(8,128)} %fine_send_h.1, s32[64,128]{1,0:T(8,128)} %fine_live_h.1, s32[1,512]{1,0:T(1,128)} %bound_h.1, s32[8,128]{1,0:T(8,128)} %bitcast.1, ...), custom_call_target="tpu_custom_call" | custom-call | tf_op jit(solution)/shard_map/pallas_call | solution.py:408
  57.4 1.7 %copy.18 = bf16[1024,128]{1,0:T(8,128)(2,1)} copy(bf16[1024,128]{1,0:T(8,128)(2,1)} %shard_map.154) | data formatting | bytes 524288

commit v2 on v0

v2 whole, which is shorter than its diff:
```python
import functools

import jax
import jax.numpy as jnp
from jax import lax
from jax.experimental import pallas as pl
from jax.experimental.pallas import tpu as pltpu
from jax.sharding import PartitionSpec as P

MESH = pl.DeviceIdType.MESH
BF = jnp.bfloat16
F32 = jnp.float32
I32 = jnp.int32


def dot(a, b):
    return jnp.dot(a, b, preferred_element_type=F32)


def dot_nt(a, b):
    return lax.dot_general(a, b, (((1,), (1,)), ((), ())), preferred_element_type=F32)


def onehot(index, rows):
    numbers = lax.broadcasted_iota(jnp.int16, (rows, index.shape[1]), 0)
    return jnp.where(numbers == index.astype(jnp.int16), jnp.ones((), BF), jnp.zeros((), BF))


def half_of(upper, folded):
    return jnp.where(upper == 1, folded[128:], folded[:128])


def centred(weight_t):
    wide = weight_t.astype(F32)
    return (wide - jnp.mean(wide, axis=0, keepdims=True)).astype(BF)


def normalised(values):
    spread = jnp.mean(values * values, axis=0, keepdims=True)
    return values * lax.rsqrt(spread + 1e-05)


def index_row(ref, block):
    rows = ref[block * 8 : block * 8 + 8, :]
    return jnp.concatenate([rows[i : i + 1, :] for i in range(8)], axis=1)


def block_lanes(block):
    return slice(block * 1024, block * 1024 + 1024)


INPUTS = (
    "nodes",
    "edge_in",
    "bound",
    "cluster",
    "fine_send",
    "fine_recv",
    "fine_edges",
    "coarse_bound",
    "edge_out",
    "fine_live",
    "node_in",
    "node_out",
    "coarse_edges",
    "coarse_recv",
    "coarse_send",
    "coarse_live",
)
SCRATCH = dict(
    state=((128, 1024), BF),
    edges_t=((128, 8192), BF),
    before=((128, 8192), F32),
    aggregate=((8, 128, 128), F32),
    recv_table=((8, 128, 128), BF),
    own_table=((256, 512), BF),
    bound_hot=((512, 512), BF),
    cluster_hot=((512, 1024), BF),
    halo_out=((2, 128, 256), BF),
    halo_in=((256, 256), BF),
    later_out=((2, 128, 256), BF),
    later_in=((2, 128, 256), BF),
    near_out=((2, 8, 256), I32),
    near_in=((2, 8, 256), I32),
    list_in=((1, 128), I32),
    count_out=((16, 512), F32),
    count_in=((3, 16, 512), F32),
    part=((2, 256, 256), BF),
    part_in=((2, 256, 256), BF),
    chip=((2, 256, 256), BF),
    chip_in=((256, 256), BF),
    mine=((2, 128, 256), BF),
    coarse_table=((2, 256, 256), BF),
    rim_out=((4, 64, 128), BF),
    rim_in=((2, 2, 64, 128), BF),
    fresh=((3, 2, 2, 128, 256), BF),
)
COPIES = (
    ["halo_l", "halo_r", "near_l", "near_r", "later_l", "later_r", "list"]
    + ["count1", "count2", "count3", "pool1", "pool2", "table"]
    + ["rim0", "rim1", "rim2", "rim3", "fresh2", "fresh1"]
    + ["ahead0", "ahead1", "ahead2", "ahead3", "back0", "back1", "back2", "back3"]
)


class Refs:
    pass


def kernel(total, *refs):
    hbm = dict(zip(INPUTS, refs))
    out_ref = refs[len(INPUTS)]
    r = Refs()
    for name, ref in zip(INPUTS + tuple(SCRATCH), refs[len(INPUTS) + 1 :]):
        setattr(r, name, ref)
    load_sem, edge_sem, send_sem, recv_sem = refs[-4:]

    me = lax.axis_index("dom")
    q = lax.rem(me, 4)
    base = me - q
    parity = lax.rem(q, 2)
    half = q // 2
    left = lax.rem(me + total - 1, total)
    right = lax.rem(me + 1, total)
    down = lax.rem(me + total - 4, total)
    up = lax.rem(me + 4, total)
    mate1 = base + q + 1 - 2 * parity
    mate2 = base + q + 2 - 4 * half
    mate3 = base + 3 - q
    mate2_down = lax.rem(mate2 + total - 4, total)
    mate2_up = lax.rem(mate2 + 4, total)
    ahead = lax.rem(base + 4, total)
    back = lax.rem(base + total - 1, total)

    def remote(name, src, dst, device, arrives=None):
        slot = COPIES.index(name)
        return pltpu.make_async_remote_copy(
            src_ref=src,
            dst_ref=dst,
            send_sem=send_sem.at[slot],
            recv_sem=recv_sem.at[slot if arrives is None else arrives],
            device_id=(device,),
            device_id_type=MESH,
        )

    barrier = pltpu.get_barrier_semaphore()

    def greet(device):
        pl.semaphore_signal(barrier, inc=1, device_id=(device,), device_id_type=MESH)

    loads = {}
    for i, name in enumerate(INPUTS):
        if name != "fine_edges":
            loads[name] = pltpu.make_async_copy(hbm[name], getattr(r, name), load_sem.at[i])

    def edge_load(b):
        rows = pl.ds(b * 1024, 1024)
        return pltpu.make_async_copy(
            hbm["fine_edges"].at[rows], r.fine_edges.at[rows], edge_sem.at[b]
        )

    loads["nodes"].start()
    loads["edge_in"].start()
    loads["bound"].start()
    loads["cluster"].start()
    for device in (left, right, mate1, mate2, mate3, down, up, mate2_down, mate2_up):
        greet(device)

    @pl.when(q == 0)
    def _():
        for i in range(4):
            greet(lax.rem(base + total - 4 + i, total))

    @pl.when(q == 3)
    def _():
        for i in range(4):
            greet(lax.rem(base + 4 + i, total))

    for name in INPUTS[4:]:
        if name == "fine_edges":
            for b in range(8):
                edge_load(b).start()
        else:
            loads[name].start()

    def own_part(layer, blocks, recv_ref, send_ref, table, edge_block):
        w_edge = r.edge_in[layer, 2].T
        for b in range(blocks):
            send = index_row(send_ref, b)
            inside = jnp.where(send < 1024, send & 511, -1)
            gathered = half_of((send >> 9) & 1, dot(table, onehot(inside, 512)))
            joined = jnp.concatenate([r.recv_table[b], w_edge], axis=1)
            columns = jnp.concatenate([onehot(index_row(recv_ref, b), 128), edge_block(b)], axis=0)
            r.before[:, block_lanes(b)] = gathered + dot(joined, columns)

    def fine_rim():
        for b in range(8):
            send = index_row(r.fine_send, b)
            outside = jnp.where(send >= 1024, send & 255, -1)
            r.before[:, block_lanes(b)] += half_of(
                (send >> 8) & 1, dot(r.halo_in[...], onehot(outside, 256))
            )

    def messages(layer, blocks, recv_ref, live_ref, keep):
        w_message = centred(r.edge_out[layer].T)
        for b in range(blocks):
            lanes = block_lanes(b)
            active = jnp.maximum(r.before[:, lanes], 0.0).astype(BF)
            message = normalised(dot(w_message, active)).astype(BF)
            if keep:
                r.edges_t[:, lanes] = (
                    r.edges_t[:, lanes].astype(F32) + message.astype(F32)
                ).astype(BF)
            target = jnp.where(index_row(live_ref, b) == 1, index_row(recv_ref, b), -1)
            r.aggregate[b] = dot_nt(message, onehot(target, 128))

    def node_update(layer, blocks, own):
        totals = jnp.concatenate([r.aggregate[b] for b in range(blocks)], axis=1)
        joined = jnp.concatenate([own, totals.astype(BF)], axis=0)
        hidden = jnp.maximum(dot(r.node_in[layer].T, joined), 0.0).astype(BF)
        change = normalised(dot(centred(r.node_out[layer].T), hidden))
        return (own.astype(F32) + change).astype(BF)

    def fine_tables(layer, own):
        table = dot(r.edge_in[layer, 1].T, own).astype(BF)
        r.own_table[:128, :] = table[:, :512]
        r.own_table[128:, :] = table[:, 512:]

    def recv_tables(layer, own, blocks):
        table = dot(r.edge_in[layer, 0].T, own).astype(BF)
        for b in range(blocks):
            r.recv_table[b] = table[:, b * 128 : (b + 1) * 128]

    def lift(group, index):
        hot = onehot(index & 511, 512)
        found = dot(r.fresh[group, 0].reshape(256, 256), hot[:256])
        found += dot(r.fresh[group, 1].reshape(256, 256), hot[256:])
        return half_of(index >> 9, found)

    for name in ("nodes", "edge_in", "bound"):
        loads[name].wait()
    r.state[...] = r.nodes[...].T
    fine_tables(0, r.state[...])
    rows = r.bound[...]
    r.bound_hot[...] = onehot(rows & 511, 512)
    picked = half_of(rows >> 9, dot(r.own_table[...], r.bound_hot[...])).astype(BF)
    r.halo_out[0] = picked[:, :256]
    r.halo_out[1] = picked[:, 256:]
    halo = (
        remote("halo_l", r.halo_out.at[0], r.halo_in.at[pl.ds(128, 128)], left),
        remote("halo_r", r.halo_out.at[1], r.halo_in.at[pl.ds(0, 128)], right),
    )

    loads["cluster"].wait()
    label = index_row(r.cluster, 0)
    digits = []
    for columns in (label[:, :512], label[:, 512:]):
        for digit in (columns & 255, columns >> 8):
            digits.append(jnp.broadcast_to(digit.astype(F32), (8, 512)).astype(BF))
    found = dot(jnp.concatenate(digits, axis=0), r.bound_hot[...])
    upper = jnp.broadcast_to(rows >> 9, (8, 512)) == 1
    low = jnp.where(upper, found[16:24], found[0:8])
    high = jnp.where(upper, found[24:32], found[8:16])
    near = (low + 256.0 * high).astype(I32)
    r.near_out[0] = near[:, :256]
    r.near_out[1] = near[:, 256:]
    r.cluster_hot[...] = onehot(label & 511, 512)
    members = lax.broadcasted_iota(I32, (16, 1024), 0) // 8 == (label >> 9)
    r.count_out[...] = dot_nt(jnp.where(members, 1.0, 0.0).astype(BF), r.cluster_hot[...])
    recv_tables(0, r.state[...], 8)
    loads["coarse_bound"].wait()

    pl.semaphore_wait(barrier, 11)
    early = halo + (
        remote("near_l", r.near_out.at[0], r.near_in.at[1], left),
        remote("near_r", r.near_out.at[1], r.near_in.at[0], right),
        remote("count1", r.count_out, r.count_in.at[0], mate1),
        remote("count2", r.count_out, r.count_in.at[1], mate2),
        remote("count3", r.count_out, r.count_in.at[2], mate3),
        remote("list", r.coarse_bound, r.list_in, mate2),
    )
    for copy in early:
        copy.start()

    loads["fine_send"].wait()
    loads["fine_recv"].wait()

    def first_edges(b):
        edge_load(b).wait()
        turned = r.fine_edges[pl.ds(b * 1024, 1024), :].T
        r.edges_t[:, block_lanes(b)] = turned
        return turned

    own_part(0, 8, r.fine_recv, r.fine_send, r.own_table[...], first_edges)
    for name in INPUTS[8:]:
        loads[name].wait()
    for copy in halo:
        copy.wait()
    fine_rim()
    messages(0, 8, r.fine_recv, r.fine_live, True)
    r.state[...] = node_update(0, 8, r.state[...])

    for copy in early[2:]:
        copy.wait()
    share = 1.0 / jnp.maximum(r.count_out[...] + r.count_in[0] + r.count_in[1] + r.count_in[2], 1.0)
    fine = r.state[...]
    nothing = jnp.zeros_like(fine)
    folded = jnp.concatenate(
        [jnp.where(label < 512, fine, nothing), jnp.where(label < 512, nothing, fine)], axis=0
    )
    sums = dot_nt(folded, r.cluster_hot[...])
    for i in range(2):
        means = (sums[i * 128 : i * 128 + 128] * share[i * 8 : i * 8 + 1]).astype(BF)
        for j in range(2):
            r.part[j, i * 128 : i * 128 + 128] = means[:, j * 256 : j * 256 + 256]
    copy = remote("pool1", r.part, r.part_in, mate1)
    copy.start()
    copy.wait()
    r.chip[...] = (r.part[...].astype(F32) + r.part_in[...].astype(F32)).astype(BF)
    pool = remote("pool2", r.chip.at[parity], r.chip_in, mate2)
    pool.start()

    rows = jnp.concatenate([r.coarse_bound[...], r.list_in[...]], axis=1)
    both = jnp.concatenate([r.chip[0], r.chip[1]], axis=1)
    picked = half_of(rows >> 9, dot(both, onehot(rows & 511, 512)))
    r.rim_out[...] = picked.T.astype(BF).reshape(4, 64, 128)
    rims = (
        remote("rim0", r.rim_out.at[0], r.rim_in.at[1, 0], down),
        remote("rim1", r.rim_out.at[1], r.rim_in.at[0, 0], up),
        remote("rim2", r.rim_out.at[2], r.rim_in.at[1, 1], mate2_down),
        remote("rim3", r.rim_out.at[3], r.rim_in.at[0, 1], mate2_up),
    )
    for copy in rims:
        copy.start()
    pool.wait()
    r.mine[...] = (
        (r.chip[parity].astype(F32) + r.chip_in[...].astype(F32)).astype(BF).reshape(2, 128, 256)
    )

    w_send = r.edge_in[1, 1].T
    for i in range(2):
        r.coarse_table[parity, i * 128 : i * 128 + 128] = dot(w_send, r.mine[i]).astype(BF)
    copy = remote("table", r.coarse_table.at[parity], r.coarse_table.at[parity], mate1)
    copy.start()
    quarter = r.mine[half]
    recv_tables(1, quarter, 2)

    table = jnp.concatenate([fine[:, :512], fine[:, 512:]], axis=0)
    picked = half_of(r.bound[...] >> 9, dot(table, r.bound_hot[...])).astype(BF)
    r.later_out[0] = picked[:, :256]
    r.later_out[1] = picked[:, 256:]
    later = (
        remote("later_l", r.later_out.at[0], r.later_in.at[1], left),
        remote("later_r", r.later_out.at[1], r.later_in.at[0], right),
    )
    copy.wait()
    for item in later:
        item.start()

    def coarse_block(b):
        return r.coarse_edges[pl.ds(b * 1024, 1024), :].T

    table = jnp.concatenate([r.coarse_table[0], r.coarse_table[1]], axis=1)
    own_part(1, 2, r.coarse_recv, r.coarse_send, table, coarse_block)
    for copy in rims:
        copy.wait()
    rim = (r.rim_in[:, 0].astype(F32) + r.rim_in[:, 1].astype(F32)).astype(BF).reshape(128, 128)
    rim_table = dot_nt(w_send, rim).astype(BF)
    for b in range(2):
        send = index_row(r.coarse_send, b)
        outside = jnp.where(send >= 1024, send & 127, -1)
        r.before[:, block_lanes(b)] += dot(rim_table, onehot(outside, 128))
    messages(1, 2, r.coarse_recv, r.coarse_live, False)

    r.fresh[1, parity, half] = node_update(1, 2, quarter)
    own = r.fresh.at[1, parity, half]
    sender = 2 * parity + half
    copy = remote("fresh2", own, own, mate2)
    copy.start()
    beside = (
        remote("ahead0", own, r.fresh.at[0, parity, half], ahead, COPIES.index("ahead0") + sender),
        remote("back0", own, r.fresh.at[2, parity, half], back, COPIES.index("back0") + sender),
    )
    for item in beside:
        item.start()
    copy.wait()
    copy = remote("fresh1", r.fresh.at[1, parity], r.fresh.at[1, parity], mate1)
    copy.start()
    copy.wait()
    r.state[...] = (r.state[...].astype(F32) + lift(1, label)).astype(BF)

    fine_tables(2, r.state[...])
    recv_tables(2, r.state[...], 8)
    own_part(
        2, 8, r.fine_recv, r.fine_send, r.own_table[...], lambda b: r.edges_t[:, block_lanes(b)]
    )
    for item in later:
        item.wait()
    for item in beside:
        item.wait_send()

    def arrive(name, group):
        for i in range(4):
            block = r.fresh.at[group, i // 2, i % 2]
            remote(name + str(i), block, block, left).wait_recv()

    @pl.when(q == 0)
    def _():
        arrive("ahead", 0)

    @pl.when(q == 3)
    def _():
        arrive("back", 2)

    w_send = r.edge_in[2, 1].T
    for side, group in ((0, jnp.where(q == 0, 0, 1)), (1, jnp.where(q == 3, 2, 1))):
        raised = lift(group, r.near_in[side][:1, :])
        rim = (r.later_in[side].astype(F32) + raised).astype(BF)
        r.halo_in[side * 128 : side * 128 + 128] = dot(w_send, rim).astype(BF)
    fine_rim()
    messages(2, 8, r.fine_recv, r.fine_live, False)
    out_ref[...] = node_update(2, 8, r.state[...]).T


def local(
    nodes,
    fine_edges,
    fine_recv,
    fine_send,
    fine_live,
    bound_rows,
    cluster,
    coarse_edges,
    coarse_recv,
    coarse_send,
    coarse_live,
    coarse_bound,
    edge_in,
    edge_out,
    node_in,
    node_out,
):
    args = dict(
        nodes=nodes,
        edge_in=edge_in,
        bound=bound_rows,
        cluster=cluster.reshape(8, 128),
        fine_send=fine_send,
        fine_recv=fine_recv,
        fine_edges=fine_edges,
        coarse_bound=coarse_bound,
        edge_out=edge_out,
        fine_live=fine_live,
        node_in=node_in,
        node_out=node_out,
        coarse_edges=coarse_edges,
        coarse_recv=coarse_recv,
        coarse_send=coarse_send,
        coarse_live=coarse_live,
    )
    held = [(args[name].shape, args[name].dtype) for name in INPUTS] + list(SCRATCH.values())
    return pl.pallas_call(
        functools.partial(kernel, lax.axis_size("dom")),
        out_shape=jax.ShapeDtypeStruct((1024, 128), BF),
        in_specs=[pl.BlockSpec(memory_space=pl.ANY)] * len(INPUTS),
        out_specs=pl.BlockSpec(memory_space=pltpu.VMEM),
        scratch_shapes=[pltpu.VMEM(shape, dtype) for shape, dtype in held]
        + [
            pltpu.SemaphoreType.DMA((len(INPUTS),)),
            pltpu.SemaphoreType.DMA((8,)),
            pltpu.SemaphoreType.DMA((len(COPIES),)),
            pltpu.SemaphoreType.DMA((len(COPIES),)),
        ],
        compiler_params=pltpu.CompilerParams(
            collective_id=0, has_side_effects=True, vmem_limit_bytes=56 << 20
        ),
    )(*[args[name] for name in INPUTS])


def solution(mesh):
    row = P("dom", None)
    return jax.shard_map(
        local,
        mesh=mesh,
        in_specs=(row,) * 6 + (P("dom"),) + (row,) * 5 + (P(),) * 4,
        out_specs=row,
        check_vma=False,
    )
```

time: 142 us -> 45.3 us (0.32)
  the two profiles are of different devices: /device:TPU:0 before, /device:TPU:1 now
where the time goes in v2:
time: 45.3 us; the launch traced here: 45.2 us
  Pallas kernels  43.5 us (96%)
  local copies, waits for them, and re-layouts  1.67 us (4%)
    pallas_call x1, Pallas kernels, local(): pl.pallas_call(functools.partial(kernel, lax.axis_size('dom')), out_shape...  43.5 us
    unnamed x1, local copies, waits for them, and re-layouts  1.67 us

profile of v2, /device:TPU:1, one launch (start us, length us, event | category | flops | bytes accessed | tf_op | source)
XLA Modules:
  0.0 45.2 jit_solution(8948958748205668504)
XLA Ops:
  0.0 43.5 %shard_map.154 = bf16[1024,128]{1,0:T(8,128)(2,1)} custom-call(bf16[1024,128]{1,0:T(8,128)(2,1)} %refs_0_.1, bf16[3,3,128,128]{3,2,1,0:T(8,128)(2,1)} %refs_1_.1, s32[1,512]{1,0:T(1,128)} %refs_2_.1, s32[8,128]{1,0:T(8,128)} %bitcast.1, s32[64,128]{1,0:T(8,128)} %refs_4_.1, s32[64,128]{1,0:T(8,128)} %refs_5_.1, bf16[8192,128]{1,0:T(8,128)(2,1)} %refs_6_.1, ...), custom_call_target="tpu_custom_call" | custom-call | tf_op jit(solution)/shard_map/pallas_call | solution.py:462
  43.5 1.7 %copy.18 = bf16[1024,128]{1,0:T(8,128)(2,1)} copy(bf16[1024,128]{1,0:T(8,128)(2,1)} %shard_map.154) | data formatting | bytes 524288

commit v3 on v2

--- a/solution.py
+++ b/solution.py
@@ -43,6 +43,10 @@
 def index_row(ref, block):
     rows = ref[block * 8 : block * 8 + 8, :]
     return jnp.concatenate([rows[i : i + 1, :] for i in range(8)], axis=1)
+
+
+def added(a, b):
+    return (a.astype(F32) + b.astype(F32)).astype(BF)
 
 
 def block_lanes(block):
@@ -80,6 +84,10 @@
     halo_in=((256, 256), BF),
     later_out=((2, 128, 256), BF),
     later_in=((2, 128, 256), BF),
+    w_edge=((3, 3, 128, 128), BF),
+    w_message=((3, 128, 128), BF),
+    w_node=((3, 128, 256), BF),
+    w_update=((3, 128, 128), BF),
     near_out=((2, 8, 256), I32),
     near_in=((2, 8, 256), I32),
     list_in=((1, 128), I32),
@@ -97,8 +105,8 @@
 )
 COPIES = (
     ["halo_l", "halo_r", "near_l", "near_r", "later_l", "later_r", "list"]
-    + ["count1", "count2", "count3", "pool1", "pool2", "table"]
-    + ["rim0", "rim1", "rim2", "rim3", "fresh2", "fresh1"]
+    + ["count1", "count2", "count3", "pool1a", "pool1b", "pool2a", "pool2b", "tablea", "tableb"]
+    + ["rim0", "rim1", "rim2", "rim3", "across", "along0", "along1"]
     + ["ahead0", "ahead1", "ahead2", "ahead3", "back0", "back1", "back2", "back3"]
 )
 
@@ -113,7 +121,7 @@
     r = Refs()
     for name, ref in zip(INPUTS + tuple(SCRATCH), refs[len(INPUTS) + 1 :]):
         setattr(r, name, ref)
-    load_sem, edge_sem, send_sem, recv_sem = refs[-4:]
+    load_sem, edge_sem, send_sem, recv_sem, here_sem = refs[-5:]
 
     me = lax.axis_index("dom")
     q = lax.rem(me, 4)
@@ -163,18 +171,8 @@
     loads["edge_in"].start()
     loads["bound"].start()
     loads["cluster"].start()
-    for device in (left, right, mate1, mate2, mate3, down, up, mate2_down, mate2_up):
+    for device in (left, right, mate1, mate2, mate3):
         greet(device)
-
-    @pl.when(q == 0)
-    def _():
-        for i in range(4):
-            greet(lax.rem(base + total - 4 + i, total))
-
-    @pl.when(q == 3)
-    def _():
-        for i in range(4):
-            greet(lax.rem(base + 4 + i, total))
 
     for name in INPUTS[4:]:
         if name == "fine_edges":
@@ -183,15 +181,22 @@
         else:
             loads[name].start()
 
-    def own_part(layer, blocks, recv_ref, send_ref, table, edge_block):
-        w_edge = r.edge_in[layer, 2].T
-        for b in range(blocks):
-            send = index_row(send_ref, b)
+    def own_part(layer):
+        w_edge = r.w_edge[layer, 2]
+        for b in range(8):
+            send = index_row(r.fine_send, b)
             inside = jnp.where(send < 1024, send & 511, -1)
-            gathered = half_of((send >> 9) & 1, dot(table, onehot(inside, 512)))
-            joined = jnp.concatenate([r.recv_table[b], w_edge], axis=1)
-            columns = jnp.concatenate([onehot(index_row(recv_ref, b), 128), edge_block(b)], axis=0)
-            r.before[:, block_lanes(b)] = gathered + dot(joined, columns)
+            gathered = half_of((send >> 9) & 1, dot(r.own_table[...], onehot(inside, 512)))
+            hot = onehot(index_row(r.fine_recv, b), 128)
+            if layer == 0:
+                edge_load(b).wait()
+                turned = r.fine_edges[pl.ds(b * 1024, 1024), :].T
+                r.edges_t[:, block_lanes(b)] = turned
+                joined = jnp.concatenate([r.recv_table[b], w_edge], axis=1)
+                rest = dot(joined, jnp.concatenate([hot, turned], axis=0))
+            else:
+                rest = r.before[:, block_lanes(b)] + dot(r.recv_table[b], hot)
+            r.before[:, block_lanes(b)] = gathered + rest
 
     def fine_rim():
         for b in range(8):
@@ -202,8 +207,8 @@
             )
 
     def messages(layer, blocks, recv_ref, live_ref, keep):
-        w_message = centred(r.edge_out[layer].T)
-        for b in range(blocks):
+        w_message = r.w_message[layer]
+        for b in blocks:
             lanes = block_lanes(b)
             active = jnp.maximum(r.before[:, lanes], 0.0).astype(BF)
             message = normalised(dot(w_message, active)).astype(BF)
@@ -215,31 +220,34 @@
             r.aggregate[b] = dot_nt(message, onehot(target, 128))
 
     def node_update(layer, blocks, own):
-        totals = jnp.concatenate([r.aggregate[b] for b in range(blocks)], axis=1)
+        totals = jnp.concatenate([r.aggregate[b] for b in blocks], axis=1)
         joined = jnp.concatenate([own, totals.astype(BF)], axis=0)
-        hidden = jnp.maximum(dot(r.node_in[layer].T, joined), 0.0).astype(BF)
-        change = normalised(dot(centred(r.node_out[layer].T), hidden))
+        hidden = jnp.maximum(dot(r.w_node[layer], joined), 0.0).astype(BF)
+        change = normalised(dot(r.w_update[layer], hidden))
         return (own.astype(F32) + change).astype(BF)
 
     def fine_tables(layer, own):
-        table = dot(r.edge_in[layer, 1].T, own).astype(BF)
+        table = dot(r.w_edge[layer, 1], own).astype(BF)
         r.own_table[:128, :] = table[:, :512]
         r.own_table[128:, :] = table[:, 512:]
 
     def recv_tables(layer, own, blocks):
-        table = dot(r.edge_in[layer, 0].T, own).astype(BF)
+        table = dot(r.w_edge[layer, 0], own).astype(BF)
         for b in range(blocks):
             r.recv_table[b] = table[:, b * 128 : (b + 1) * 128]
 
+    def lifting(group, side):
+        return r.fresh[group, side].reshape(256, 256)
+
     def lift(group, index):
         hot = onehot(index & 511, 512)
-        found = dot(r.fresh[group, 0].reshape(256, 256), hot[:256])
-        found += dot(r.fresh[group, 1].reshape(256, 256), hot[256:])
+        found = dot(lifting(group, 0), hot[:256]) + dot(lifting(group, 1), hot[256:])
         return half_of(index >> 9, found)
 
     for name in ("nodes", "edge_in", "bound"):
         loads[name].wait()
     r.state[...] = r.nodes[...].T
+    r.w_edge[0, 1] = r.edge_in[0, 1].T
     fine_tables(0, r.state[...])
     rows = r.bound[...]
     r.bound_hot[...] = onehot(rows & 511, 512)
@@ -250,6 +258,12 @@
         remote("halo_l", r.halo_out.at[0], r.halo_in.at[pl.ds(128, 128)], left),
         remote("halo_r", r.halo_out.at[1], r.halo_in.at[pl.ds(0, 128)], right),
     )
+
+    pl.semaphore_wait(barrier, 5)
+    for copy in halo:
+        copy.start()
+    r.w_edge[0, 0] = r.edge_in[0, 0].T
+    r.w_edge[0, 2] = r.edge_in[0, 2].T
 
     loads["cluster"].wait()
     label = index_row(r.cluster, 0)
@@ -269,9 +283,7 @@
     r.count_out[...] = dot_nt(jnp.where(members, 1.0, 0.0).astype(BF), r.cluster_hot[...])
     recv_tables(0, r.state[...], 8)
     loads["coarse_bound"].wait()
-
-    pl.semaphore_wait(barrier, 11)
-    early = halo + (
+    early = (
         remote("near_l", r.near_out.at[0], r.near_in.at[1], left),
         remote("near_r", r.near_out.at[1], r.near_in.at[0], right),
         remote("count1", r.count_out, r.count_in.at[0], mate1),
@@ -285,22 +297,29 @@
     loads["fine_send"].wait()
     loads["fine_recv"].wait()
 
-    def first_edges(b):
-        edge_load(b).wait()
-        turned = r.fine_edges[pl.ds(b * 1024, 1024), :].T
-        r.edges_t[:, block_lanes(b)] = turned
-        return turned
-
-    own_part(0, 8, r.fine_recv, r.fine_send, r.own_table[...], first_edges)
+    own_part(0)
     for name in INPUTS[8:]:
         loads[name].wait()
+    for layer in range(3):
+        if layer:
+            for i in range(3):
+                r.w_edge[layer, i] = r.edge_in[layer, i].T
+        r.w_message[layer] = centred(r.edge_out[layer].T)
+        r.w_node[layer] = r.node_in[layer].T
+        r.w_update[layer] = centred(r.node_out[layer].T)
     for copy in halo:
         copy.wait()
+
+    @pl.when((q == 0) | (q == 3))
+    def _():
+        for device in (mate1, mate2, mate3):
+            pl.semaphore_signal(here_sem, inc=1, device_id=(device,), device_id_type=MESH)
+
     fine_rim()
-    messages(0, 8, r.fine_recv, r.fine_live, True)
-    r.state[...] = node_update(0, 8, r.state[...])
-
-    for copy in early[2:]:
+    messages(0, range(8), r.fine_recv, r.fine_live, True)
+    r.state[...] = node_update(0, range(8), r.state[...])
+
+    for copy in early:
         copy.wait()
     share = 1.0 / jnp.maximum(r.count_out[...] + r.count_in[0] + r.count_in[1] + r.count_in[2], 1.0)
     fine = r.state[...]
@@ -313,12 +332,20 @@
         means = (sums[i * 128 : i * 128 + 128] * share[i * 8 : i * 8 + 1]).astype(BF)
         for j in range(2):
             r.part[j, i * 128 : i * 128 + 128] = means[:, j * 256 : j * 256 + 256]
-    copy = remote("pool1", r.part, r.part_in, mate1)
-    copy.start()
-    copy.wait()
-    r.chip[...] = (r.part[...].astype(F32) + r.part_in[...].astype(F32)).astype(BF)
-    pool = remote("pool2", r.chip.at[parity], r.chip_in, mate2)
-    pool.start()
+    other = 1 - parity
+    first = remote("pool1a", r.part.at[other], r.part_in.at[other], mate1)
+    second = remote("pool1b", r.part.at[parity], r.part_in.at[parity], mate1)
+    first.start()
+    second.start()
+    first.wait()
+    r.chip[parity] = added(r.part[parity], r.part_in[parity])
+    pool = []
+    for i in range(2):
+        rows = pl.ds(i * 128, 128)
+        pool.append(remote("pool2" + "ab"[i], r.chip.at[parity, rows], r.chip_in.at[rows], mate2))
+        pool[i].start()
+    second.wait()
+    r.chip[other] = added(r.part[other], r.part_in[other])
 
     rows = jnp.concatenate([r.coarse_bound[...], r.list_in[...]], axis=1)
     both = jnp.concatenate([r.chip[0], r.chip[1]], axis=1)
@@ -330,18 +357,28 @@
         remote("rim2", r.rim_out.at[2], r.rim_in.at[1, 1], mate2_down),
         remote("rim3", r.rim_out.at[3], r.rim_in.at[0, 1], mate2_up),
     )
+
+    @pl.when((q == 0) | (q == 3))
+    def _():
+        pl.semaphore_wait(here_sem, 1)
+
+    @pl.when((q == 1) | (q == 2))
+    def _():
+        pl.semaphore_wait(here_sem, 2)
+
     for copy in rims:
         copy.start()
-    pool.wait()
-    r.mine[...] = (
-        (r.chip[parity].astype(F32) + r.chip_in[...].astype(F32)).astype(BF).reshape(2, 128, 256)
-    )
-
-    w_send = r.edge_in[1, 1].T
+
+    w_send = r.w_edge[1, 1]
+    tables = []
     for i in range(2):
-        r.coarse_table[parity, i * 128 : i * 128 + 128] = dot(w_send, r.mine[i]).astype(BF)
-    copy = remote("table", r.coarse_table.at[parity], r.coarse_table.at[parity], mate1)
-    copy.start()
+        pool[i].wait()
+        rows = slice(i * 128, i * 128 + 128)
+        r.mine[i] = added(r.chip[parity, rows], r.chip_in[rows])
+        r.coarse_table[parity, rows] = dot(w_send, r.mine[i]).astype(BF)
+        block = r.coarse_table.at[parity, pl.ds(i * 128, 128)]
+        tables.append(remote("table" + "ab"[i], block, block, mate1))
+        tables[i].start()
     quarter = r.mine[half]
     recv_tables(1, quarter, 2)
 
@@ -353,15 +390,25 @@
         remote("later_l", r.later_out.at[0], r.later_in.at[1], left),
         remote("later_r", r.later_out.at[1], r.later_in.at[0], right),
     )
-    copy.wait()
     for item in later:
         item.start()
 
-    def coarse_block(b):
-        return r.coarse_edges[pl.ds(b * 1024, 1024), :].T
-
-    table = jnp.concatenate([r.coarse_table[0], r.coarse_table[1]], axis=1)
-    own_part(1, 2, r.coarse_recv, r.coarse_send, table, coarse_block)
+    def coarse_part(b, side):
+        send = index_row(r.coarse_send, b)
+        inside = jnp.where(((send >> 8) & 1) == side, send & 255, -1)
+        hot = onehot(jnp.where(send < 1024, inside, -1), 256)
+        return half_of((send >> 9) & 1, dot(r.coarse_table[side], hot))
+
+    w_edge = r.w_edge[1, 2]
+    for b in range(2):
+        joined = jnp.concatenate([r.recv_table[b], w_edge], axis=1)
+        turned = r.coarse_edges[pl.ds(b * 1024, 1024), :].T
+        columns = jnp.concatenate([onehot(index_row(r.coarse_recv, b), 128), turned], axis=0)
+        r.before[:, block_lanes(b)] = dot(joined, columns) + coarse_part(b, parity)
+    for item in tables:
+        item.wait()
+    for b in range(2):
+        r.before[:, block_lanes(b)] += coarse_part(b, other)
     for copy in rims:
         copy.wait()
     rim = (r.rim_in[:, 0].astype(F32) + r.rim_in[:, 1].astype(F32)).astype(BF).reshape(128, 128)
@@ -370,30 +417,37 @@
         send = index_row(r.coarse_send, b)
         outside = jnp.where(send >= 1024, send & 127, -1)
         r.before[:, block_lanes(b)] += dot(rim_table, onehot(outside, 128))
-    messages(1, 2, r.coarse_recv, r.coarse_live, False)
-
-    r.fresh[1, parity, half] = node_update(1, 2, quarter)
+
+    messages(1, range(2), r.coarse_recv, r.coarse_live, False)
+    r.fresh[1, parity, half] = node_update(1, range(2), quarter)
     own = r.fresh.at[1, parity, half]
     sender = 2 * parity + half
-    copy = remote("fresh2", own, own, mate2)
-    copy.start()
+    across = remote("across", own, own, mate2)
+    along = remote("along0", own, own, mate1)
+    across.start()
+    along.start()
     beside = (
         remote("ahead0", own, r.fresh.at[0, parity, half], ahead, COPIES.index("ahead0") + sender),
         remote("back0", own, r.fresh.at[2, parity, half], back, COPIES.index("back0") + sender),
     )
     for item in beside:
         item.start()
-    copy.wait()
-    copy = remote("fresh1", r.fresh.at[1, parity], r.fresh.at[1, parity], mate1)
-    copy.start()
-    copy.wait()
-    r.state[...] = (r.state[...].astype(F32) + lift(1, label)).astype(BF)
+    w_edge = r.w_edge[2, 2]
+    for b in range(8):
+        r.before[:, block_lanes(b)] = dot(w_edge, r.edges_t[:, block_lanes(b)])
+    across.wait()
+    block = r.fresh.at[1, parity, 1 - half]
+    forward = remote("along1", block, block, mate1)
+    forward.start()
+    found = dot(lifting(1, parity), r.cluster_hot[pl.ds(pl.multiple_of(parity * 256, 256), 256)])
+    along.wait()
+    forward.wait()
+    found += dot(lifting(1, other), r.cluster_hot[pl.ds(pl.multiple_of(other * 256, 256), 256)])
+    r.state[...] = (r.state[...].astype(F32) + half_of(label >> 9, found)).astype(BF)
 
     fine_tables(2, r.state[...])
     recv_tables(2, r.state[...], 8)
-    own_part(
-        2, 8, r.fine_recv, r.fine_send, r.own_table[...], lambda b: r.edges_t[:, block_lanes(b)]
-    )
+    own_part(2)
     for item in later:
         item.wait()
     for item in beside:
@@ -412,14 +466,14 @@
     def _():
         arrive("back", 2)
 
-    w_send = r.edge_in[2, 1].T
+    w_send = r.w_edge[2, 1]
     for side, group in ((0, jnp.where(q == 0, 0, 1)), (1, jnp.where(q == 3, 2, 1))):
         raised = lift(group, r.near_in[side][:1, :])
         rim = (r.later_in[side].astype(F32) + raised).astype(BF)
         r.halo_in[side * 128 : side * 128 + 128] = dot(w_send, rim).astype(BF)
     fine_rim()
-    messages(2, 8, r.fine_recv, r.fine_live, False)
-    out_ref[...] = node_update(2, 8, r.state[...]).T
+    messages(2, range(8), r.fine_recv, r.fine_live, False)
+    out_ref[...] = node_update(2, range(8), r.state[...]).T
 
 
 def local(
@@ -470,6 +524,7 @@
             pltpu.SemaphoreType.DMA((8,)),
             pltpu.SemaphoreType.DMA((len(COPIES),)),
             pltpu.SemaphoreType.DMA((len(COPIES),)),
+            pltpu.SemaphoreType.REGULAR,
         ],
         compiler_params=pltpu.CompilerParams(
             collective_id=0, has_side_effects=True, vmem_limit_bytes=56 << 20

time: 45.3 us -> 44.5 us (0.982)
  Pallas kernels: 43.5 us -> 42.7 us
    pallas_call x1, Pallas kernels: 43.5 us -> 42.7 us  [local(): pl.pallas_call(functools.partial(kernel, lax.axis_size('dom')), out_shape...]
where the time goes in v3:
time: 44.5 us; the launch traced here: 44.4 us
  Pallas kernels  42.7 us (96%)
  local copies, waits for them, and re-layouts  1.67 us (4%)
    pallas_call x1, Pallas kernels, local(): pl.pallas_call(functools.partial(kernel, lax.axis_size('dom')), out_shape...  42.7 us
    unnamed x1, local copies, waits for them, and re-layouts  1.67 us

profile of v3, /device:TPU:1, one launch (start us, length us, event | category | flops | bytes accessed | tf_op | source)
XLA Modules:
  0.0 44.4 jit_solution(6268196922680490494)
XLA Ops:
  0.0 42.7 %shard_map.154 = bf16[1024,128]{1,0:T(8,128)(2,1)} custom-call(bf16[1024,128]{1,0:T(8,128)(2,1)} %refs_0_.1, bf16[3,3,128,128]{3,2,1,0:T(8,128)(2,1)} %refs_1_.1, s32[1,512]{1,0:T(1,128)} %refs_2_.1, s32[8,128]{1,0:T(8,128)} %bitcast.1, s32[64,128]{1,0:T(8,128)} %refs_4_.1, s32[64,128]{1,0:T(8,128)} %refs_5_.1, bf16[8192,128]{1,0:T(8,128)(2,1)} %refs_6_.1, ...), custom_call_target="tpu_custom_call" | custom-call | tf_op jit(solution)/shard_map/pallas_call | solution.py:516
  42.7 1.7 %copy.18 = bf16[1024,128]{1,0:T(8,128)(2,1)} copy(bf16[1024,128]{1,0:T(8,128)(2,1)} %shard_map.154) | data formatting | bytes 524288

commit v4 on v3

--- a/solution.py
+++ b/solution.py
@@ -88,6 +88,10 @@
     w_message=((3, 128, 128), BF),
     w_node=((3, 128, 256), BF),
     w_update=((3, 128, 128), BF),
+    digits=((32, 512), BF),
+    sender_cluster=((8, 1024), F32),
+    later_sums=((128, 8192), F32),
+    lift_table=((2, 256, 256), BF),
     near_out=((2, 8, 256), I32),
     near_in=((2, 8, 256), I32),
     list_in=((1, 128), I32),
@@ -158,7 +162,7 @@
 
     loads = {}
     for i, name in enumerate(INPUTS):
-        if name != "fine_edges":
+        if name not in ("fine_edges", "edge_in"):
             loads[name] = pltpu.make_async_copy(hbm[name], getattr(r, name), load_sem.at[i])
 
     def edge_load(b):
@@ -167,36 +171,74 @@
             hbm["fine_edges"].at[rows], r.fine_edges.at[rows], edge_sem.at[b]
         )
 
+    first_weights = pltpu.make_async_copy(
+        hbm["edge_in"].at[0], r.edge_in.at[0], load_sem.at[len(INPUTS)]
+    )
+    loads["edge_in"] = pltpu.make_async_copy(
+        hbm["edge_in"].at[pl.ds(1, 2)], r.edge_in.at[pl.ds(1, 2)], load_sem.at[1]
+    )
     loads["nodes"].start()
-    loads["edge_in"].start()
+    first_weights.start()
     loads["bound"].start()
     loads["cluster"].start()
     for device in (left, right, mate1, mate2, mate3):
         greet(device)
 
-    for name in INPUTS[4:]:
-        if name == "fine_edges":
-            for b in range(8):
-                edge_load(b).start()
-        else:
-            loads[name].start()
-
-    def own_part(layer):
-        w_edge = r.w_edge[layer, 2]
+    def first_sums():
+        w_edge = r.w_edge[0, 2]
         for b in range(8):
             send = index_row(r.fine_send, b)
             inside = jnp.where(send < 1024, send & 511, -1)
             gathered = half_of((send >> 9) & 1, dot(r.own_table[...], onehot(inside, 512)))
-            hot = onehot(index_row(r.fine_recv, b), 128)
-            if layer == 0:
-                edge_load(b).wait()
-                turned = r.fine_edges[pl.ds(b * 1024, 1024), :].T
-                r.edges_t[:, block_lanes(b)] = turned
-                joined = jnp.concatenate([r.recv_table[b], w_edge], axis=1)
-                rest = dot(joined, jnp.concatenate([hot, turned], axis=0))
-            else:
-                rest = r.before[:, block_lanes(b)] + dot(r.recv_table[b], hot)
-            r.before[:, block_lanes(b)] = gathered + rest
+            edge_load(b).wait()
+            turned = r.fine_edges[pl.ds(b * 1024, 1024), :].T
+            r.edges_t[:, block_lanes(b)] = turned
+            joined = jnp.concatenate([r.recv_table[b], w_edge], axis=1)
+            columns = jnp.concatenate([onehot(index_row(r.fine_recv, b), 128), turned], axis=0)
+            r.before[:, block_lanes(b)] = gathered + dot(joined, columns)
+
+    def digits_of(upper, found):
+        low = jnp.where(upper == 1, found[16:17], found[0:1])
+        high = jnp.where(upper == 1, found[24:25], found[8:9])
+        return low + 256.0 * high
+
+    def later_own(blocks):
+        table = jnp.concatenate([r.own_table[...], r.digits[...]], axis=0)
+        for b in blocks:
+            send = index_row(r.fine_send, b)
+            upper = (send >> 9) & 1
+            found = dot(table, onehot(jnp.where(send < 1024, send & 511, -1), 512))
+            r.sender_cluster[b : b + 1, :] = digits_of(upper, found[256:])
+            r.later_sums[:, block_lanes(b)] = half_of(upper, found[:256]) + dot(
+                r.w_edge[2, 2], r.edges_t[:, block_lanes(b)]
+            )
+
+    def later_rim():
+        near = r.near_in[...]
+        digits = []
+        for i in range(2):
+            for digit in (near[i] & 255, near[i] >> 8):
+                digits.append(digit.astype(F32).astype(BF))
+        table = jnp.concatenate([r.halo_in[...]] + digits, axis=0)
+        for b in range(8):
+            send = index_row(r.fine_send, b)
+            upper = (send >> 8) & 1
+            found = dot(table, onehot(jnp.where(send >= 1024, send & 255, -1), 256))
+            r.sender_cluster[b : b + 1, :] += digits_of(upper, found[256:])
+            r.later_sums[:, block_lanes(b)] += half_of(upper, found[:256])
+
+    def lifted_sums():
+        table = jnp.concatenate([r.lift_table[0], r.lift_table[1]], axis=1)
+        for b in range(8):
+            place = index_row(r.fine_send, b) >> 8
+            cluster = r.sender_cluster[b : b + 1, :].astype(I32)
+            beside = ((place == 4) & (q == 0)) | ((place == 5) & (q == 3))
+            found = dot(table, onehot(jnp.where(beside, -1, cluster & 511), 512))
+            r.before[:, block_lanes(b)] = (
+                r.later_sums[:, block_lanes(b)]
+                + half_of(cluster >> 9, found)
+                + dot(r.recv_table[b], onehot(index_row(r.fine_recv, b), 128))
+            )
 
     def fine_rim():
         for b in range(8):
@@ -239,13 +281,25 @@
     def lifting(group, side):
         return r.fresh[group, side].reshape(256, 256)
 
+    def raise_table(side):
+        for i in range(2):
+            rows = slice(i * 128, i * 128 + 128)
+            r.lift_table[side, rows] = dot(r.w_edge[2, 1], r.fresh[1, side, i]).astype(BF)
+
     def lift(group, index):
         hot = onehot(index & 511, 512)
         found = dot(lifting(group, 0), hot[:256]) + dot(lifting(group, 1), hot[256:])
         return half_of(index >> 9, found)
 
-    for name in ("nodes", "edge_in", "bound"):
-        loads[name].wait()
+    loads["nodes"].wait()
+    first_weights.wait()
+    loads["bound"].wait()
+    for name in INPUTS[4:] + ("edge_in",):
+        if name == "fine_edges":
+            for b in range(8):
+                edge_load(b).start()
+        else:
+            loads[name].start()
     r.state[...] = r.nodes[...].T
     r.w_edge[0, 1] = r.edge_in[0, 1].T
     fine_tables(0, r.state[...])
@@ -271,7 +325,8 @@
     for columns in (label[:, :512], label[:, 512:]):
         for digit in (columns & 255, columns >> 8):
             digits.append(jnp.broadcast_to(digit.astype(F32), (8, 512)).astype(BF))
-    found = dot(jnp.concatenate(digits, axis=0), r.bound_hot[...])
+    r.digits[...] = jnp.concatenate(digits, axis=0)
+    found = dot(r.digits[...], r.bound_hot[...])
     upper = jnp.broadcast_to(rows >> 9, (8, 512)) == 1
     low = jnp.where(upper, found[16:24], found[0:8])
     high = jnp.where(upper, found[24:32], found[8:16])
@@ -297,8 +352,8 @@
     loads["fine_send"].wait()
     loads["fine_recv"].wait()
 
-    own_part(0)
-    for name in INPUTS[8:]:
+    first_sums()
+    for name in INPUTS[8:] + ("edge_in",):
         loads[name].wait()
     for layer in range(3):
         if layer:
@@ -369,6 +424,19 @@
     for copy in rims:
         copy.start()
 
+    table = jnp.concatenate([fine[:, :512], fine[:, 512:]], axis=0)
+    picked = half_of(r.bound[...] >> 9, dot(table, r.bound_hot[...])).astype(BF)
+    r.later_out[0] = picked[:, :256]
+    r.later_out[1] = picked[:, 256:]
+    later = (
+        remote("later_l", r.later_out.at[0], r.later_in.at[1], left),
+        remote("later_r", r.later_out.at[1], r.later_in.at[0], right),
+    )
+    for item in later:
+        item.start()
+    fine_tables(2, fine)
+    later_own(range(4))
+
     w_send = r.w_edge[1, 1]
     tables = []
     for i in range(2):
@@ -381,17 +449,6 @@
         tables[i].start()
     quarter = r.mine[half]
     recv_tables(1, quarter, 2)
-
-    table = jnp.concatenate([fine[:, :512], fine[:, 512:]], axis=0)
-    picked = half_of(r.bound[...] >> 9, dot(table, r.bound_hot[...])).astype(BF)
-    r.later_out[0] = picked[:, :256]
-    r.later_out[1] = picked[:, 256:]
-    later = (
-        remote("later_l", r.later_out.at[0], r.later_in.at[1], left),
-        remote("later_r", r.later_out.at[1], r.later_in.at[0], right),
-    )
-    for item in later:
-        item.start()
 
     def coarse_part(b, side):
         send = index_row(r.coarse_send, b)
@@ -432,24 +489,26 @@
     )
     for item in beside:
         item.start()
-    w_edge = r.w_edge[2, 2]
-    for b in range(8):
-        r.before[:, block_lanes(b)] = dot(w_edge, r.edges_t[:, block_lanes(b)])
+    later_own(range(4, 8))
+    for item in later:
+        item.wait()
+    for i in range(2):
+        r.halo_in[i * 128 : i * 128 + 128] = dot(r.w_edge[2, 1], r.later_in[i]).astype(BF)
+    later_rim()
     across.wait()
     block = r.fresh.at[1, parity, 1 - half]
     forward = remote("along1", block, block, mate1)
     forward.start()
+    raise_table(parity)
     found = dot(lifting(1, parity), r.cluster_hot[pl.ds(pl.multiple_of(parity * 256, 256), 256)])
     along.wait()
     forward.wait()
+    raise_table(other)
     found += dot(lifting(1, other), r.cluster_hot[pl.ds(pl.multiple_of(other * 256, 256), 256)])
     r.state[...] = (r.state[...].astype(F32) + half_of(label >> 9, found)).astype(BF)
 
-    fine_tables(2, r.state[...])
     recv_tables(2, r.state[...], 8)
-    own_part(2)
-    for item in later:
-        item.wait()
+    lifted_sums()
     for item in beside:
         item.wait_send()
 
@@ -466,12 +525,16 @@
     def _():
         arrive("back", 2)
 
-    w_send = r.w_edge[2, 1]
-    for side, group in ((0, jnp.where(q == 0, 0, 1)), (1, jnp.where(q == 3, 2, 1))):
-        raised = lift(group, r.near_in[side][:1, :])
-        rim = (r.later_in[side].astype(F32) + raised).astype(BF)
-        r.halo_in[side * 128 : side * 128 + 128] = dot(w_send, rim).astype(BF)
-    fine_rim()
+    @pl.when((q == 0) | (q == 3))
+    def _():
+        side = jnp.where(q == 0, 0, 1)
+        raised = lift(2 * side, r.near_in[side][:1, :]).astype(BF)
+        table = dot(r.w_edge[2, 1], raised).astype(BF)
+        for b in range(8):
+            send = index_row(r.fine_send, b)
+            outside = jnp.where((send >> 8) == 4 + side, send & 255, -1)
+            r.before[:, block_lanes(b)] += dot(table, onehot(outside, 256))
+
     messages(2, range(8), r.fine_recv, r.fine_live, False)
     out_ref[...] = node_update(2, range(8), r.state[...]).T
 
@@ -520,7 +583,7 @@
         out_specs=pl.BlockSpec(memory_space=pltpu.VMEM),
         scratch_shapes=[pltpu.VMEM(shape, dtype) for shape, dtype in held]
         + [
-            pltpu.SemaphoreType.DMA((len(INPUTS),)),
+            pltpu.SemaphoreType.DMA((len(INPUTS) + 1,)),
             pltpu.SemaphoreType.DMA((8,)),
             pltpu.SemaphoreType.DMA((len(COPIES),)),
             pltpu.SemaphoreType.DMA((len(COPIES),)),

time: 44.5 us -> 43 us (0.966)
  Pallas kernels: 42.7 us -> 41.2 us
    pallas_call x1, Pallas kernels: 42.7 us -> 41.2 us  [local(): pl.pallas_call(functools.partial(kernel, lax.axis_size('dom')), out_shape...]
where the time goes in v4:
time: 43 us; the launch traced here: 42.9 us
  Pallas kernels  41.2 us (96%)
  local copies, waits for them, and re-layouts  1.67 us (4%)
    pallas_call x1, Pallas kernels, local(): pl.pallas_call(functools.partial(kernel, lax.axis_size('dom')), out_shape...  41.2 us
    unnamed x1, local copies, waits for them, and re-layouts  1.67 us

profile of v4, /device:TPU:1, one launch (start us, length us, event | category | flops | bytes accessed | tf_op | source)
XLA Modules:
  0.0 42.9 jit_solution(4249658560767513072)
XLA Ops:
  0.0 41.2 %shard_map.154 = bf16[1024,128]{1,0:T(8,128)(2,1)} custom-call(bf16[1024,128]{1,0:T(8,128)(2,1)} %refs_0_.1, bf16[3,3,128,128]{3,2,1,0:T(8,128)(2,1)} %refs_1_.1, s32[1,512]{1,0:T(1,128)} %refs_2_.1, s32[8,128]{1,0:T(8,128)} %bitcast.1, s32[64,128]{1,0:T(8,128)} %refs_4_.1, s32[64,128]{1,0:T(8,128)} %refs_5_.1, bf16[8192,128]{1,0:T(8,128)(2,1)} %refs_6_.1, ...), custom_call_target="tpu_custom_call" | custom-call | tf_op jit(solution)/shard_map/pallas_call | solution.py:579
  41.2 1.7 %copy.18 = bf16[1024,128]{1,0:T(8,128)(2,1)} copy(bf16[1024,128]{1,0:T(8,128)(2,1)} %shard_map.154) | data formatting | bytes 524288

commit v5 on v4

--- a/solution.py
+++ b/solution.py
@@ -487,9 +487,9 @@
         remote("ahead0", own, r.fresh.at[0, parity, half], ahead, COPIES.index("ahead0") + sender),
         remote("back0", own, r.fresh.at[2, parity, half], back, COPIES.index("back0") + sender),
     )
+    later_own(range(4, 8))
     for item in beside:
         item.start()
-    later_own(range(4, 8))
     for item in later:
         item.wait()
     for i in range(2):

time: 43 us -> 43 us (level)
  no operation moved by 1% of the time
where the time goes in v5:
time: 43 us; the launch traced here: 42.9 us
  Pallas kernels  41.2 us (96%)
  local copies, waits for them, and re-layouts  1.67 us (4%)
    pallas_call x1, Pallas kernels, local(): pl.pallas_call(functools.partial(kernel, lax.axis_size('dom')), out_shape...  41.2 us
    unnamed x1, local copies, waits for them, and re-layouts  1.67 us

profile of v5, /device:TPU:1, one launch (start us, length us, event | category | flops | bytes accessed | tf_op | source)
XLA Modules:
  0.0 42.9 jit_solution(14919422499342103618)
XLA Ops:
  0.0 41.2 %shard_map.154 = bf16[1024,128]{1,0:T(8,128)(2,1)} custom-call(bf16[1024,128]{1,0:T(8,128)(2,1)} %refs_0_.1, bf16[3,3,128,128]{3,2,1,0:T(8,128)(2,1)} %refs_1_.1, s32[1,512]{1,0:T(1,128)} %refs_2_.1, s32[8,128]{1,0:T(8,128)} %bitcast.1, s32[64,128]{1,0:T(8,128)} %refs_4_.1, s32[64,128]{1,0:T(8,128)} %refs_5_.1, bf16[8192,128]{1,0:T(8,128)(2,1)} %refs_6_.1, ...), custom_call_target="tpu_custom_call" | custom-call | tf_op jit(solution)/shard_map/pallas_call | solution.py:579
  41.2 1.7 %copy.18 = bf16[1024,128]{1,0:T(8,128)(2,1)} copy(bf16[1024,128]{1,0:T(8,128)(2,1)} %shard_map.154) | data formatting | bytes 524288

commit v6 on v5

--- a/solution.py
+++ b/solution.py
@@ -110,7 +110,7 @@
 COPIES = (
     ["halo_l", "halo_r", "near_l", "near_r", "later_l", "later_r", "list"]
     + ["count1", "count2", "count3", "pool1a", "pool1b", "pool2a", "pool2b", "tablea", "tableb"]
-    + ["rim0", "rim1", "rim2", "rim3", "across", "along0", "along1"]
+    + ["rim0", "rim1", "rim2", "rim3", "across0", "across1", "along0", "along1", "along2"]
     + ["ahead0", "ahead1", "ahead2", "ahead3", "back0", "back1", "back2", "back3"]
 )
 
@@ -479,9 +479,13 @@
     r.fresh[1, parity, half] = node_update(1, range(2), quarter)
     own = r.fresh.at[1, parity, half]
     sender = 2 * parity + half
-    across = remote("across", own, own, mate2)
+    pieces = [pl.ds(i * 64, 64) for i in range(2)]
+    across = []
+    for i, rows in enumerate(pieces):
+        piece = r.fresh.at[1, parity, half, rows]
+        across.append(remote("across" + str(i), piece, piece, mate2))
+        across[i].start()
     along = remote("along0", own, own, mate1)
-    across.start()
     along.start()
     beside = (
         remote("ahead0", own, r.fresh.at[0, parity, half], ahead, COPIES.index("ahead0") + sender),
@@ -495,14 +499,17 @@
     for i in range(2):
         r.halo_in[i * 128 : i * 128 + 128] = dot(r.w_edge[2, 1], r.later_in[i]).astype(BF)
     later_rim()
-    across.wait()
-    block = r.fresh.at[1, parity, 1 - half]
-    forward = remote("along1", block, block, mate1)
-    forward.start()
+    forward = []
+    for i, rows in enumerate(pieces):
+        across[i].wait()
+        piece = r.fresh.at[1, parity, 1 - half, rows]
+        forward.append(remote("along" + str(i + 1), piece, piece, mate1))
+        forward[i].start()
     raise_table(parity)
     found = dot(lifting(1, parity), r.cluster_hot[pl.ds(pl.multiple_of(parity * 256, 256), 256)])
     along.wait()
-    forward.wait()
+    for item in forward:
+        item.wait()
     raise_table(other)
     found += dot(lifting(1, other), r.cluster_hot[pl.ds(pl.multiple_of(other * 256, 256), 256)])
     r.state[...] = (r.state[...].astype(F32) + half_of(label >> 9, found)).astype(BF)

time: 43 us -> 43 us (level)
  no operation moved by 1% of the time
where the time goes in v6:
time: 43 us; the launch traced here: 42.9 us
  Pallas kernels  41.2 us (96%)
  local copies, waits for them, and re-layouts  1.67 us (4%)
    pallas_call x1, Pallas kernels, local(): pl.pallas_call(functools.partial(kernel, lax.axis_size('dom')), out_shape...  41.2 us
    unnamed x1, local copies, waits for them, and re-layouts  1.67 us

profile of v6, /device:TPU:1, one launch (start us, length us, event | category | flops | bytes accessed | tf_op | source)
XLA Modules:
  0.0 42.9 jit_solution(5416805638075658131)
XLA Ops:
  0.0 41.2 %shard_map.154 = bf16[1024,128]{1,0:T(8,128)(2,1)} custom-call(bf16[1024,128]{1,0:T(8,128)(2,1)} %refs_0_.1, bf16[3,3,128,128]{3,2,1,0:T(8,128)(2,1)} %refs_1_.1, s32[1,512]{1,0:T(1,128)} %refs_2_.1, s32[8,128]{1,0:T(8,128)} %bitcast.1, s32[64,128]{1,0:T(8,128)} %refs_4_.1, s32[64,128]{1,0:T(8,128)} %refs_5_.1, bf16[8192,128]{1,0:T(8,128)(2,1)} %refs_6_.1, ...), custom_call_target="tpu_custom_call" | custom-call | tf_op jit(solution)/shard_map/pallas_call | solution.py:586
  41.2 1.7 %copy.18 = bf16[1024,128]{1,0:T(8,128)(2,1)} copy(bf16[1024,128]{1,0:T(8,128)(2,1)} %shard_map.154) | data formatting | bytes 524288
